TPU v7x, 256 devices: a whole 4x4x8 slice. The times are simulated.
256 devices in a mesh: row: 16 (over y_lo, x, core), col: 16 (over z, y_hi).
Axes of the slice: x: 4, y: 4 (y_hi: 2, y_lo: 2; y = y_hi * 2 + y_lo), z: 8, core: 2. Of those that a mesh axis runs over, the one named last changes fastest.
Arguments:
- pair_act: bfloat16 [512, 512, 128], P('row', 'col'), may hold values from -6 to 6
- out_grad: bfloat16 [512, 512, 128], P('row', 'col'), may hold values from -6 to 6
- valid_count: int32 [1], replicated, may hold values from 128 to 511
- w_in: bfloat16 [128, 640], replicated, may hold values from -0.5 to 0.5
- w_out: bfloat16 [128, 128], replicated, may hold values from -0.5 to 0.5
- in_gain: float32 [128], replicated, may hold values from 0.5 to 1.5
- in_bias: float32 [128], replicated, may hold values from -3 to 3
- out_gain: float32 [128], replicated, may hold values from 0.5 to 1.5
- out_bias: float32 [128], replicated, may hold values from -3 to 3
Outputs:
- grad_pair: bfloat16 [512, 512, 128], P('row', 'col')
- grad_in: float32 [128, 640], replicated
- grad_out: float32 [128, 128], replicated
All inputs are finite; a program needn't handle non-finite values.
Results may differ from a plain program's by a relative error of at most 0.02.
Values may be sent and summed in bfloat16 or wider, within the bound.
No kernel may reach another device: no remote copies, remote signals or barrier semaphores. Data moves between devices by JAX's collectives and lax.ppermute only.
A program may use at most 128 MiB of HBM per device.

v0:
```python
import jax
import jax.numpy as jnp
from jax import lax
from jax.sharding import PartitionSpec as P

EPS = 1e-05


def norm_forward(values, gain, bias):
    mean = jnp.mean(values, axis=-1, keepdims=True)
    centred = values - mean
    rstd = lax.rsqrt(jnp.mean(centred * centred, axis=-1, keepdims=True) + EPS)
    unit = centred * rstd
    return (unit * gain + bias, unit, rstd)


def norm_backward(grad, unit, rstd, gain):
    scaled = grad * gain
    first = jnp.mean(scaled, axis=-1, keepdims=True)
    second = jnp.mean(scaled * unit, axis=-1, keepdims=True)
    return rstd * (scaled - first - unit * second)


def shards(pair_act, out_grad, valid_count, w_in, w_out, in_gain, in_bias, out_gain, out_bias):
    f32 = jnp.float32
    bf16 = jnp.bfloat16
    rows = pair_act.shape[0]
    cols = pair_act.shape[1]
    hidden = w_out.shape[0]
    total = rows * lax.axis_size("row")
    row_first = lax.axis_index("row") * rows
    col_first = lax.axis_index("col") * cols
    row_valid = (row_first + jnp.arange(rows) < valid_count[0]).astype(f32)
    col_valid = (col_first + jnp.arange(cols) < valid_count[0]).astype(f32)
    both = row_valid[:, None, None] * col_valid[None, :, None]
    normed, z_unit, z_rstd = norm_forward(pair_act.astype(f32), in_gain, in_bias)
    normed16 = normed.astype(bf16)
    proj = jnp.einsum("ijc,cd->ijd", normed16, w_in, preferred_element_type=f32)
    left_val = proj[..., :hidden]
    left_sig = jax.nn.sigmoid(proj[..., hidden : 2 * hidden])
    right_val = proj[..., 2 * hidden : 3 * hidden]
    right_sig = jax.nn.sigmoid(proj[..., 3 * hidden : 4 * hidden])
    gate = jax.nn.sigmoid(proj[..., 4 * hidden :])
    left16 = (left_sig * left_val * both).astype(bf16)
    right16 = (right_sig * right_val * both).astype(bf16)
    right_strip = lax.all_gather(right16, "row", axis=0, tiled=True)
    part = right_strip
    tri = jnp.swapaxes(
        lax.psum_scatter(
            jnp.einsum("ikh,jkh->jih", left16, part, preferred_element_type=f32).astype(
                jnp.bfloat16
            ),
            "col",
            scatter_dimension=0,
            tiled=True,
        ).astype(jnp.float32),
        0,
        1,
    )
    tri_norm, tri_unit, tri_rstd = norm_forward(tri, out_gain, out_bias)
    tri16 = tri_norm.astype(bf16)
    projected = jnp.einsum("ijh,hc->ijc", tri16, w_out, preferred_element_type=f32)
    cotangent = out_grad.astype(f32)
    scaled16 = (cotangent * gate).astype(bf16)
    gate_grad = cotangent * projected * gate * (1.0 - gate)
    out_local = jnp.einsum("ijh,ijc->hc", tri16, scaled16, preferred_element_type=f32)
    tri_back = jnp.einsum("ijc,hc->ijh", scaled16, w_out, preferred_element_type=f32)
    tri_grad16 = norm_backward(tri_back, tri_unit, tri_rstd, out_gain).astype(bf16)
    grad_strip = lax.all_gather(tri_grad16, "col", axis=1, tiled=True)
    left_grad = jnp.einsum("ijh,jkh->ikh", grad_strip, right_strip, preferred_element_type=f32)
    part = grad_strip
    right_grad = lax.psum_scatter(
        jnp.einsum("ijh,ikh->jkh", part, left16, preferred_element_type=f32).astype(jnp.bfloat16),
        "row",
        scatter_dimension=0,
        tiled=True,
    ).astype(jnp.float32)
    proj_grad16 = jnp.concatenate(
        [
            left_grad * both * left_sig,
            left_grad * both * left_val * left_sig * (1.0 - left_sig),
            right_grad * both * right_sig,
            right_grad * both * right_val * right_sig * (1.0 - right_sig),
            gate_grad,
        ],
        axis=-1,
    ).astype(bf16)
    in_local = jnp.einsum("ijc,ijd->cd", normed16, proj_grad16, preferred_element_type=f32)
    normed_grad = jnp.einsum("ijd,cd->ijc", proj_grad16, w_in, preferred_element_type=f32)
    grad_pair = norm_backward(normed_grad, z_unit, z_rstd, in_gain).astype(bf16)
    in_total, out_total = lax.psum((in_local, out_local), ("row", "col"))
    return (grad_pair, in_total / total, out_total / total)


def solution(mesh):
    return jax.shard_map(
        shards,
        mesh=mesh,
        in_specs=(P("row", "col", None), P("row", "col", None), P(), P(), P(), P(), P(), P(), P()),
        out_specs=(P("row", "col", None), P(), P()),
        check_vma=False,
    )
```

profile of v0, /device:TPU:1, one launch (start us, length us, event | category | flops | bytes accessed | tf_op | source)
XLA Modules:
  0.0 754.3 jit_solution(6973288600539459413)
XLA Ops:
  7.2 0.0 copy-start
  7.2 0.0 copy-start.4
  7.2 0.0 all-gather.3.cloned.1.call-start
  8.0 1.2 convert_reduce_fusion
  9.1 1.3 fusion.15
  10.5 0.1 broadcast_multiply_fusion.2
  10.6 0.0 copy-done
  10.6 1.6 fusion.43
  12.1 0.0 copy-done.4
  12.2 1.1 multiply_convert_fusion.4
  13.3 0.0 all-gather.3.cloned.1.call-update
  13.3 0.0 reduce-scatter.3.cloned.1.call-start
  13.4 2.6 copy.29
  16.0 41.6 %all-gather.3.cloned.1.call-done = bf16[512,32,128]{2,1,0:T(8,128)(2,1)} async-done(((bf16[32,32,128]{2,1,0:T(8,128)(2,1)}), bf16[512,32,128]{2,1,0:T(8,128)(2,1)}) %all-gather.3.cloned.1.call-update) | async-done | bytes 4194320 | tf_op jit(solution)/shard_map/all_gather | solution.py:46
  57.6 8.5 %copy.26 = bf16[512,32,128]{0,1,2:T(8,128)(2,1)} copy(bf16[512,32,128]{2,1,0:T(8,128)(2,1)} %all-gather.3.cloned.1.call-done) | data formatting | bytes 8388608 | tf_op jit(solution)/shard_map/all_gather | solution.py:46
  66.1 5.9 convert_bitcast_fusion.1
  72.0 9.1 %copy.23 = bf16[512,32,128]{2,1,0:T(8,128)(2,1)} copy(bf16[512,32,128]{0,1,2:T(8,128)(2,1)} %convert_bitcast_fusion.1) | data formatting | bytes 8388608 | tf_op jit(solution)/shard_map/convert_element_type | solution.py:50
  81.1 0.0 copy-start.6
  81.1 0.0 copy-start.9
  81.1 0.0 copy-start.10
  81.1 0.0 reduce-scatter.3.cloned.1.call-update
  81.1 0.0 all-gather.5.cloned.1.call-start
  81.2 207.5 %reduce-scatter.3.cloned.1.call-done = bf16[32,32,128]{2,1,0:T(8,128)(2,1)} async-done(((bf16[512,32,128]{2,1,0:T(8,128)(2,1)}), bf16[32,32,128]{2,1,0:T(8,128)(2,1)}) %reduce-scatter.3.cloned.1.call-update) | async-done | bytes 262160 | tf_op jit(solution)/shard_map/reduce_scatter | solution.py:49
  288.7 1.2 bitcast_reduce_fusion
  289.9 1.3 fusion.37
  291.3 0.0 copy-done.6
  291.3 0.0 copy-done.9
  291.3 0.0 copy-done.10
  291.3 1.6 fusion.52
  292.9 1.6 fusion.34
  294.5 0.8 copy.25
  295.3 0.0 all-gather.5.cloned.1.call-update
  295.3 0.0 reduce-scatter.5.cloned.1.call-start
  295.4 99.4 %all-gather.5.cloned.1.call-done = bf16[32,512,128]{2,0,1:T(8,128)(2,1)} async-done(((bf16[32,32,128]{2,0,1:T(8,128)(2,1)}), bf16[32,512,128]{2,0,1:T(8,128)(2,1)}) %all-gather.5.cloned.1.call-update) | async-done | bytes 4194320 | tf_op jit(solution)/shard_map/all_gather | solution.py:69
  394.8 8.6 %copy.27 = bf16[32,512,128]{1,0,2:T(8,128)(2,1)} copy(bf16[32,512,128]{2,0,1:T(8,128)(2,1)} %all-gather.5.cloned.1.call-done) | data formatting | bytes 8388608 | tf_op jit(solution)/shard_map/all_gather | solution.py:69
  403.4 5.7 fusion.54
  409.1 9.1 %copy.31 = bf16[128,32,512]{0,1,2:T(8,128)(2,1)} copy(bf16[128,32,512]{2,1,0:T(8,128)(2,1)} %fusion.54) | data formatting | bytes 8388608 | tf_op jit(solution)/shard_map/ijh,ikh->jkh/dot_general | solution.py:73
  418.3 0.0 copy-start.2
  418.3 0.0 copy-start.11
  418.3 0.0 reduce-scatter.5.cloned.1.call-update
  418.3 0.2 all-reduce.3.cloned.1.call-start
  418.5 0.7 copy-done.2
  419.2 0.0 copy-done.11
  419.2 1.2 convolution_bitcast_fusion.1
  420.4 6.0 fusion.53
  426.4 2.8 copy.28
  429.2 1.0 fusion.38
  430.2 0.9 fusion.39
  431.1 52.8 %reduce-scatter.5.cloned.1.call-done = bf16[32,32,128]{2,1,0:T(8,128)(2,1)} async-done(((bf16[512,32,128]{2,1,0:T(8,128)(2,1)}), bf16[32,32,128]{2,1,0:T(8,128)(2,1)}) %reduce-scatter.5.cloned.1.call-update) | async-done | bytes 262160 | tf_op jit(solution)/shard_map/reduce_scatter | solution.py:72
  483.9 1.9 fusion.40
  485.9 2.0 fusion.41
  487.9 0.0 copy-done.3
  487.9 0.0 copy-done.5
  487.9 1.2 fusion.3
  489.1 0.0 copy-done.1
  489.1 0.0 copy-done.7
  489.1 0.0 copy-done.8
  489.1 2.8 convolution_bitcast_fusion
  491.9 2.0 fusion.51
  494.0 0.0 all-reduce.3.cloned.1.call-update
  494.0 1.3 fusion.14
  495.3 249.3 %all-reduce.3.cloned.1.call-done = (f32[128,640]{1,0:T(8,128)}, f32[128,128]{1,0:T(8,128)}) async-done(((f32[128,640]{1,0:T(8,128)}, f32[128,128]{1,0:T(8,128)}), (f32[128,640]{1,0:T(8,128)}, f32[128,128]{1,0:T(8,128)})) %all-reduce.3.cloned.1.call-update) | async-done | bytes 393232 | tf_op jit(solution)/shard_map/psum | solution.py:91
  744.6 1.7 broadcast_multiply_fusion
  746.3 1.5 broadcast_multiply_fusion.1
  (14 shorter events, 0.1 us)
Async XLA Ops:
  7.2 3.4 copy-start
  7.2 5.0 copy-start.4
  7.2 50.4 %all-gather.3.cloned.1.call-start = ((), (), s32[]{:S(2)}) async-start(), calls=%async_computation.2 | async-start | bytes 4456448 | tf_op jit(solution)/shard_map/all_gather | solution.py:46
  13.3 275.4 %reduce-scatter.3.cloned.1.call-start = ((), (), s32[]{:S(2)}) async-start(), calls=%async_computation.3 | async-start | bytes 4456448 | tf_op jit(solution)/shard_map/reduce_scatter | solution.py:49
  81.1 210.2 %copy-start.6 = (bf16[32,32,128]{2,1,0:T(8,128)(2,1)S(1)}, bf16[32,32,128]{2,1,0:T(8,128)(2,1)}, u32[]{:S(2)}) copy-start(bf16[32,32,128]{2,1,0:T(8,128)(2,1)} %get-tuple-element.11) | copy-start | bytes 786436
  81.1 210.2 %copy-start.9 = (bf16[128,128]{1,0:T(8,128)(2,1)S(1)}, bf16[128,128]{1,0:T(8,128)(2,1)}, u32[]{:S(2)}) copy-start(bf16[128,128]{1,0:T(8,128)(2,1)} %param.13) | copy-start | bytes 98308
  81.1 210.2 %copy-start.10 = (f32[128]{0:T(128)S(1)}, f32[128]{0:T(128)}, u32[]{:S(2)}) copy-start(f32[128]{0:T(128)} %param.16) | copy-start | bytes 1540
  81.1 313.7 %all-gather.5.cloned.1.call-start = ((), (), s32[]{:S(2)}) async-start(), calls=%async_computation.4 | async-start | bytes 4456448 | tf_op jit(solution)/shard_map/all_gather | solution.py:69
  295.3 188.6 %reduce-scatter.5.cloned.1.call-start = ((), (), s32[]{:S(2)}) async-start(), calls=%async_computation.5 | async-start | bytes 4456448 | tf_op jit(solution)/shard_map/reduce_scatter | solution.py:72
  418.3 0.9 copy-start.2
  418.3 1.0 copy-start.11
  418.3 326.3 %all-reduce.3.cloned.1.call-start = ((), (), s32[]{:S(2)}) async-start(), calls=%async_computation.6 | async-start | bytes 786432 | tf_op jit(solution)/shard_map/psum | solution.py:91
  431.1 56.7 %copy-start.3 = (bf16[32,32,128]{2,1,0:T(8,128)(2,1)S(1)}, bf16[32,32,128]{2,1,0:T(8,128)(2,1)}, u32[]{:S(2)}) copy-start(bf16[32,32,128]{2,1,0:T(8,128)(2,1)} %reduce-scatter.3.cloned.1.call-done) | copy-start | bytes 786436
  483.9 3.9 copy-start.5
  485.9 3.2 copy-start.1
  485.9 3.2 copy-start.7
  485.9 3.2 copy-start.8
Sparse Core Ops, SparseCore 0:
  13.4 44.0 all-gather.2
  81.3 207.4 reduce-scatter.2
  295.5 99.3 all-gather.4
  418.4 65.4 reduce-scatter.4
  494.1 250.4 all-reduce.2
where the time goes:
time: 756 us; the launch traced here: 754 us
  waiting for transfers between devices  651 us (86%)
  local copies, waits for them, and re-layouts  42.4 us (6%)
  matrix products  28 us (4%)
  other arithmetic  18.1 us (2%)
  between operations  14.7 us (2%)
    psum x1, waiting for transfers between devices, shards(): in_total, out_total = lax.psum((in_local, out_local), ('row', 'col'))  249 us
    reduce_scatter x1, waiting for transfers between devices, shards(): lax.psum_scatter(jnp.einsum('ikh,jkh->jih', left16, part, preferred_eleme...  208 us
    all_gather x1, waiting for transfers between devices, shards(): grad_strip = lax.all_gather(tri_grad16, 'col', axis=1, tiled=True)  99.4 us
    reduce_scatter x1, waiting for transfers between devices, shards(): lax.psum_scatter(jnp.einsum('ijh,ikh->jkh', part, left16, preferred_eleme...  52.8 us
    all_gather x1, waiting for transfers between devices, shards(): right_strip = lax.all_gather(right16, 'row', axis=0, tiled=True)  41.6 us
  transfers between devices with their start and end apart: 5, of which 5 were waited for; matrix products, arithmetic and copies ran while one was open for 2% of the time, Pallas kernels for 0%

commit v1 on v0

v1 whole, which is shorter than its diff:
```python
import functools

import jax
import jax.numpy as jnp
from jax import lax
from jax.experimental import pallas as pl
from jax.experimental.pallas import tpu as pltpu
from jax.sharding import Mesh
from jax.sharding import PartitionSpec as P

EPS = 1e-05
F32 = jnp.float32
BF16 = jnp.bfloat16
ROW = ("rh", "core")
CHIPS = ("rh", "col")
VMEM = pl.BlockSpec(memory_space=pltpu.VMEM)
SMEM = pl.BlockSpec(memory_space=pltpu.SMEM)


def column(ref):
    wide = jnp.broadcast_to(ref[...], (128, 128)).T
    return jnp.concatenate([wide, wide], axis=1)


def dot(a, b, dims):
    return lax.dot_general(a, b, ((dims[:1], dims[1:]), ((), ())), preferred_element_type=F32)


def norm_unit(values):
    mean = jnp.sum(values, axis=0, keepdims=True) * (1.0 / 128)
    centred = values - mean
    var = jnp.sum(centred * centred, axis=0, keepdims=True) * (1.0 / 128)
    rstd = lax.rsqrt(var + EPS)
    return centred * rstd, rstd


def norm_backward(grad, unit, rstd, gain):
    scaled = grad * gain
    first = jnp.sum(scaled, axis=0, keepdims=True) * (1.0 / 128)
    second = jnp.sum(scaled * unit, axis=0, keepdims=True) * (1.0 / 128)
    return rstd * (scaled - first - unit * second)


def pair_mask(valid, n):
    lane = lax.broadcasted_iota(jnp.int32, (1, 256), 1)
    first = 8 * ((lane // 32) % 4) + 2 * n + lane // 128
    row = 32 * (2 * lax.axis_index("rh") + lax.axis_index("core")) + first
    col = 32 * lax.axis_index("col") + lane % 32
    return ((row < valid) & (col < valid)).astype(F32)


def load_t(ref, n):
    return jnp.concatenate(
        [ref[:, q].reshape(128, 128).astype(F32).T for q in (2 * n, 2 * n + 1)], axis=1
    )


def load_strided(ref, n, first, stride):
    return jnp.concatenate(
        [ref[pl.ds(first + q, 128, stride=stride), :] for q in (2 * n, 2 * n + 1)], axis=1
    )


def store_strided(ref, n, first, stride, values):
    for d in range(2):
        ref[pl.ds(first + 2 * n + d, 128, stride=stride), :] = values[:, 128 * d : 128 * d + 128]


def swap_groups(parts):
    lane = lax.broadcasted_iota(jnp.int32, parts[0].shape, 1)
    low, even = lane < 64, lane % 64 < 32
    mid = [None] * 4
    for f in range(2):
        x, y = parts[f], parts[f + 2]
        mid[f] = jnp.where(low, x, pltpu.roll(y, 64, 1))
        mid[f + 2] = jnp.where(low, pltpu.roll(x, 64, 1), y)
    out = [None] * 4
    for f in (0, 2):
        x, y = mid[f], mid[f + 1]
        out[f] = jnp.where(even, x, pltpu.roll(y, 32, 1))
        out[f + 1] = jnp.where(even, pltpu.roll(x, 96, 1), y)
    return out


def project_kernel(valid_ref, x_ref, w_ref, gain_ref, bias_ref, xt_ref, nt_ref, lr_ref, scr):
    gain, bias = column(gain_ref), column(bias_ref)
    for n in range(4):
        x = load_t(x_ref, n)
        lanes = slice(256 * n, 256 * n + 256)
        xt_ref[:, lanes] = x.astype(BF16)
        unit, _ = norm_unit(x)
        normed = (unit * gain + bias).astype(BF16)
        nt_ref[:, lanes] = normed
        proj = dot(w_ref[:, :512], normed, (0, 0))
        mask = pair_mask(valid_ref[0], n)
        left = jax.nn.sigmoid(proj[128:256]) * proj[:128] * mask
        right = jax.nn.sigmoid(proj[384:512]) * proj[256:384] * mask
        store_strided(scr, n, 0, 16, left)
        store_strided(scr, n, 8, 16, right)
    lr_ref[...] = scr[...].reshape(128, 16, 128).astype(BF16)


def triangle_kernel(own_ref, other_ref, mats_ref, tri_ref):
    me = lax.axis_index("core")
    for ref, core in ((own_ref, me), (other_ref, 1 - me)):
        for t in range(4):
            parts = [
                ref[:, 4 * t + f].astype(F32).reshape(128, 128) for f in range(4)
            ]
            rows = [y.reshape(8, 2, 8, 128) for y in swap_groups(parts)]
            for side in range(2):
                for h in range(2):
                    pair = jnp.concatenate([rows[2 * h][:, side], rows[2 * h + 1][:, side]], axis=1)
                    mats_ref[side, :, core, 16 * h : 16 * h + 16, 128 * t : 128 * t + 128] = (
                        pair.astype(BF16)
                    )
    left = mats_ref[0, :, me].reshape(256, 512)
    right = mats_ref[1].reshape(512, 512)
    tri = dot(left, right, (1, 1)).reshape(8, 4, 8, 512)
    for t in range(4):
        parts = [tri[:, a, :, 128 * t : 128 * t + 128].reshape(64, 128) for a in range(4)]
        cols = [x.reshape(8, 8, 128) for x in swap_groups(parts)]
        for h in range(2):
            tri_ref[:, 2 * t + h] = jnp.concatenate(
                [cols[2 * h], cols[2 * h + 1]], axis=1
            ).astype(BF16)


def output_kernel(
    tri_ref, nt_ref, og_ref, w_ref, wo_ref, gain_ref, bias_ref, tg_ref, gg_ref, ol_ref, scr
):
    gain, bias = column(gain_ref), column(bias_ref)
    scr[...] = tri_ref[...].astype(F32).reshape(1024, 128)
    total = None
    for n in range(4):
        lanes = slice(256 * n, 256 * n + 256)
        unit, rstd = norm_unit(load_strided(scr, n, 0, 8))
        tri = (unit * gain + bias).astype(BF16)
        projected = dot(wo_ref[...], tri, (0, 0))
        gate = jax.nn.sigmoid(dot(w_ref[:, 512:640], nt_ref[:, lanes], (0, 0)))
        cotangent = load_t(og_ref, n)
        scaled = (cotangent * gate).astype(BF16)
        gg_ref[:, lanes] = (cotangent * projected * gate * (1.0 - gate)).astype(BF16)
        local = dot(tri, scaled, (1, 1))
        total = local if total is None else total + local
        back = dot(wo_ref[...], scaled, (1, 0))
        store_strided(scr, n, 0, 8, norm_backward(back, unit, rstd, gain))
    ol_ref[...] = total
    tg_ref[...] = scr[...].reshape(64, 16, 128).astype(BF16)


def triangle_back_kernel(own_ref, other_ref, mats_ref, out_ref, tg, rg):
    me = lax.axis_index("core")
    for ref, core in ((own_ref, me), (other_ref, 1 - me)):
        for t in range(4):
            parts = []
            for h in range(2):
                both = ref[:, 2 * t + h].astype(F32)
                parts += [both[:, :8].reshape(64, 128), both[:, 8:].reshape(64, 128)]
            rows = [y.reshape(8, 8, 128) for y in swap_groups(parts)]
            for h in range(2):
                tg[:, core, 16 * h : 16 * h + 16, 128 * t : 128 * t + 128] = jnp.concatenate(
                    [rows[2 * h], rows[2 * h + 1]], axis=1
                ).astype(BF16)
    right = mats_ref[1].reshape(512, 512)
    left_grad = dot(tg[:, me].reshape(256, 512), right, (1, 0)).reshape(8, 4, 8, 512)
    left = mats_ref[0].reshape(512, 512)
    rg[...] = dot(tg[...].reshape(512, 512), left, (0, 0)).reshape(8, 2, 32, 512)
    right_grad = rg[:, me].reshape(8, 4, 8, 512)
    for t in range(4):
        cols = []
        for grad in (left_grad, right_grad):
            parts = [grad[:, a, :, 128 * t : 128 * t + 128].reshape(64, 128) for a in range(4)]
            cols.append([x.reshape(8, 8, 128) for x in swap_groups(parts)])
        for f in range(4):
            out_ref[:, 4 * t + f] = jnp.concatenate([cols[0][f], cols[1][f]], axis=1).astype(BF16)


def input_kernel(
    valid_ref, grads_ref, gg_ref, xt_ref, w_ref, gain_ref, bias_ref, gp_ref, il_ref, scr
):
    gain, bias = column(gain_ref), column(bias_ref)
    scr[...] = grads_ref[...].astype(F32).reshape(2048, 128)
    total = None
    for n in range(4):
        lanes = slice(256 * n, 256 * n + 256)
        unit, rstd = norm_unit(xt_ref[:, lanes].astype(F32))
        normed = (unit * gain + bias).astype(BF16)
        proj = dot(w_ref[:, :512], normed, (0, 0))
        mask = pair_mask(valid_ref[0], n)
        pieces = []
        for side in range(2):
            val = proj[256 * side : 256 * side + 128]
            sig = jax.nn.sigmoid(proj[256 * side + 128 : 256 * side + 256])
            grad = load_strided(scr, n, 8 * side, 16) * mask * sig
            pieces += [grad.astype(BF16), (grad * val * (1.0 - sig)).astype(BF16)]
        pieces.append(gg_ref[:, lanes])
        proj_grad = jnp.concatenate(pieces, axis=0)
        local = dot(normed, proj_grad, (1, 1))
        total = local if total is None else total + local
        back = dot(w_ref[...], proj_grad, (1, 0))
        grad = norm_backward(back, unit, rstd, gain)
        for d in range(2):
            gp_ref[:, 2 * n + d] = (
                grad[:, 128 * d : 128 * d + 128].T.astype(BF16).reshape(4, 32, 128)
            )
    for b in range(5):
        il_ref[b] = total[:, 128 * b : 128 * b + 128]


def call(kernel, outs, specs, scratch=()):
    return pl.pallas_call(
        kernel,
        out_shape=[jax.ShapeDtypeStruct(s, d) for s, d in outs],
        in_specs=specs,
        out_specs=[VMEM] * len(outs),
        scratch_shapes=[pltpu.VMEM(s, d) for s, d in scratch],
        compiler_params=pltpu.CompilerParams(vmem_limit_bytes=48 * 1024 * 1024),
    )


def spread(block, axes, n):
    return lax.all_to_all(jnp.broadcast_to(block[None], (n,) + block.shape), axes, 0, 0, tiled=True)


def sum_everywhere(values):
    mine = lax.all_to_all(values.astype(BF16).reshape(16, 48, 128), ROW, 0, 0, tiled=True)
    mine = jnp.sum(mine.astype(F32), axis=0).astype(BF16)
    mine = jnp.sum(spread(mine, "col", 16).astype(F32), axis=0).astype(BF16)
    return spread(mine, ROW, 16).reshape(768, 128).astype(F32)


def other_core(x):
    return lax.ppermute(x, "core", [(0, 1), (1, 0)])


def shards(pair_act, out_grad, valid_count, w_in, w_out, in_gain, in_bias, out_gain, out_bias):
    gains = [g.reshape(1, 128) for g in (in_gain, in_bias, out_gain, out_bias)]
    x_t, normed_t, lr = call(
        project_kernel,
        [((128, 1024), BF16), ((128, 1024), BF16), ((128, 16, 128), BF16)],
        [SMEM] + [VMEM] * 4,
        [((2048, 128), F32)],
    )(valid_count, pair_act.reshape(4, 8, 32, 128), w_in, gains[0], gains[1])
    own = lax.all_to_all(lr, CHIPS, 0, 0, tiled=True)
    other = other_core(own)
    mats, tri = call(
        triangle_kernel,
        [((2, 8, 2, 32, 512), BF16), ((8, 8, 16, 128), BF16)],
        [VMEM] * 2,
    )(own.reshape(8, 16, 16, 128), other.reshape(8, 16, 16, 128))
    tri = lax.all_to_all(tri.reshape(128, 8, 128), CHIPS, 0, 0, tiled=True)
    tri_grad, gate_grad, out_local = call(
        output_kernel,
        [((64, 16, 128), BF16), ((128, 1024), BF16), ((128, 128), F32)],
        [VMEM] * 7,
        [((1024, 128), F32)],
    )(
        tri.reshape(64, 16, 128),
        normed_t,
        out_grad.reshape(4, 8, 32, 128),
        w_in,
        w_out,
        gains[2],
        gains[3],
    )
    own = lax.all_to_all(tri_grad.reshape(128, 8, 128), CHIPS, 0, 0, tiled=True)
    other = other_core(own)
    (grads,) = call(
        triangle_back_kernel,
        [((8, 16, 16, 128), BF16)],
        [VMEM] * 3,
        [((8, 2, 32, 512), BF16), ((8, 2, 32, 512), F32)],
    )(own.reshape(8, 8, 16, 128), other.reshape(8, 8, 16, 128), mats)
    grads = lax.all_to_all(grads.reshape(128, 16, 128), CHIPS, 0, 0, tiled=True)
    grad_pair, in_local = call(
        input_kernel,
        [((4, 8, 32, 128), BF16), ((5, 128, 128), F32)],
        [SMEM] + [VMEM] * 6,
        [((2048, 128), F32)],
    )(valid_count, grads, gate_grad, x_t, w_in, gains[0], gains[1])
    local = jnp.concatenate([in_local.reshape(640, 128), out_local], axis=0)
    total = sum_everywhere(local) * (1.0 / 512)
    grad_in = jnp.swapaxes(total[:640].reshape(5, 128, 128), 0, 1).reshape(128, 640)
    return grad_pair.reshape(32, 32, 128), grad_in, total[640:]


def solution(mesh):
    fine = Mesh(mesh.devices.reshape(8, 2, 16), ("rh", "core", "col"))
    pairs = P(ROW, "col", None)
    return jax.shard_map(
        shards,
        mesh=fine,
        in_specs=(pairs, pairs, P(), P(), P(), P(), P(), P(), P()),
        out_specs=(pairs, P(), P()),
        check_vma=False,
    )
```

time: 756 us -> 160 us (0.21)
  waiting for transfers between devices: 651 us -> 19 us
  blocking collectives: 0 us -> 112 us
  local copies, waits for them, and re-layouts: 42.4 us -> 4.96 us
  matrix products: 28 us -> 0 us
  other arithmetic: 18.1 us -> 0.15 us
  between operations: 14.7 us -> 1.41 us
  starting transfers between devices: 0.39 us -> 13.4 us
  Pallas kernels: 0 us -> 8.88 us
    reduce_scatter x2 -> x0, waiting for transfers between devices: 260 us -> none  [the longest x1 208 us: shards(): lax.psum_scatter(jnp.einsum('ikh,jkh->jih', left16, part, preferred_eleme...]
    psum x1 -> x0, waiting for transfers between devices: 249 us -> none  [shards(): in_total, out_total = lax.psum((in_local, out_local), ('row', 'col'))]
    all_gather x2 -> x0, waiting for transfers between devices: 141 us -> none  [the longest x1 99.4 us: shards(): grad_strip = lax.all_gather(tri_grad16, 'col', axis=1, tiled=True)]
    all_to_all x0 -> x6, blocking collectives: none -> 112 us  [the longest x1 32.3 us: shards(): own = lax.all_to_all(lr, CHIPS, 0, 0, tiled=True)]
    dot_general x9 -> x0, matrix products: 28 us -> none  [the longest x1 6 us: shards(): jnp.einsum('ijh,jkh->ikh', grad_strip, right_strip, preferred_element_typ...]
    all_gather x2 -> x0, local copies, waits for them, and re-layouts: 17.2 us -> none  [the longest x1 8.62 us: shards(): grad_strip = lax.all_gather(tri_grad16, 'col', axis=1, tiled=True)]
    all_to_all x0 -> x1, waiting for transfers between devices: none -> 16.3 us  [shards(): grads = lax.all_to_all(grads.reshape(128, 16, 128), CHIPS, 0, 0, tiled=True)]
    convert_element_type x3 -> x0, local copies, waits for them, and re-layouts: 12.5 us -> none  [the longest x1 9.12 us: shards(): jnp.einsum('ikh,jkh->jih', left16, part, preferred_element_type=f32)]
  transfers between devices with their start and end apart: 5 -> 3, of which waited for: 5 -> 3; matrix products, arithmetic and copies ran while one was open for 2% -> 0% of each run, Pallas kernels for 0% -> 0%
where the time goes in v1:
time: 160 us
  blocking collectives  112 us (70%)
  waiting for transfers between devices  19 us (12%)
  starting transfers between devices  13.4 us (8%)
  Pallas kernels  8.88 us (6%)
  local copies, waits for them, and re-layouts  4.96 us (3%)
    all_to_all x1, blocking collectives, shards(): own = lax.all_to_all(lr, CHIPS, 0, 0, tiled=True)  32.3 us
    all_to_all x2, blocking collectives, spread(): lax.all_to_all(jnp.broadcast_to(block[None], (n,) + block.shape), axes, 0...  26.6 us
    all_to_all x1, blocking collectives, shards(): own = lax.all_to_all(tri_grad.reshape(128, 8, 128), CHIPS, 0, 0, tiled=True)  20.1 us
    all_to_all x1, blocking collectives, shards(): tri = lax.all_to_all(tri.reshape(128, 8, 128), CHIPS, 0, 0, tiled=True)  19.5 us
    all_to_all x1, waiting for transfers between devices, shards(): grads = lax.all_to_all(grads.reshape(128, 16, 128), CHIPS, 0, 0, tiled=True)  16.3 us
    all_to_all x1, blocking collectives, sum_everywhere(): lax.all_to_all(values.astype(BF16).reshape(16, 48, 128), ROW, 0, 0, tiled...  13.6 us
    all_to_all x1, starting transfers between devices, shards(): grads = lax.all_to_all(grads.reshape(128, 16, 128), CHIPS, 0, 0, tiled=True)  7.18 us
    ppermute x2, starting transfers between devices, other_core(): return lax.ppermute(x, 'core', [(0, 1), (1, 0)])  6.22 us
  transfers between devices with their start and end apart: 3, of which 3 were waited for; matrix products, arithmetic and copies ran while one was open for 0% of the time, Pallas kernels for 0%

profile of v1, /device:TPU:1, one launch (start us, length us, event | category | flops | bytes accessed | tf_op | source)
XLA Modules:
  0.0 159.8 jit_solution(9293070857734769723)
XLA Ops:
  1.3 0.0 copy-start.5
  1.3 0.0 copy-start.6
  1.3 0.6 copy-done.5
  1.9 0.0 copy-done.6
  1.9 0.0 copy-start
  2.0 0.9 copy-done
  2.9 0.0 copy-start.3
  2.9 0.9 copy-done.3
  3.8 0.8 shard_map.112
  4.6 32.3 %all_to_all.35 = bf16[128,16,128]{2,1,0:T(8,128)(2,1)S(1)} all-to-all(bf16[128,16,128]{2,1,0:T(8,128)(2,1)S(1)} %get-tuple-element.13), channel_id=1, replica_groups=mesh['rh'=8,'core'=2,'col'=16] {'rh','col'}, dimensions={0} | all-to-all | bytes 1048576 | tf_op jit(solution)/shard_map/all_to_all | solution.py:245
  36.9 2.8 %collective-permute-start = (bf16[128,16,128]{2,1,0:T(8,128)(2,1)S(1)}, bf16[128,16,128]{2,1,0:T(8,128)(2,1)S(1)}, u32[]{:S(2)}, u32[]{:S(2)}) collective-permute-start(bf16[128,16,128]{2,1,0:T(8,128)(2,1)S(1)} %all_to_all.35), channel_id=1, source_target_pairs={{0,16},{16,0},{1,17},{17,1},{2,18},{18,2},{3,19},{19,3},{4,20},{20... | collective-permute-start | bytes 1572872 | tf_op jit(solution)/shard_map/ppermute | solution.py:234
  39.7 1.5 collective-permute-done
  41.2 1.8 %shard_map.113 = (bf16[2,8,2,32,512]{4,3,2,1,0:T(8,128)(2,1)S(1)}, bf16[8,8,16,128]{3,2,1,0:T(8,128)(2,1)S(1)}) custom-call(bf16[8,16,16,128]{3,2,1,0:T(8,128)(2,1)S(1)} %bitcast.22, bf16[8,16,16,128]{3,2,1,0:T(8,128)(2,1)S(1)} %bitcast.25), custom_call_target="tpu_custom_call" | custom-call | tf_op jit(solution)/shard_map/pallas_call | solution.py:247
  43.0 0.0 copy-start.1
  43.0 0.0 copy-start.2
  43.0 0.0 copy-start.4
  43.1 19.5 %all_to_all.36 = bf16[128,8,128]{2,1,0:T(8,128)(2,1)S(1)} all-to-all(bf16[128,8,128]{2,1,0:T(8,128)(2,1)S(1)} %bitcast.29), channel_id=1, replica_groups=mesh['rh'=8,'core'=2,'col'=16] {'rh','col'}, dimensions={0} | all-to-all | bytes 524288 | tf_op jit(solution)/shard_map/all_to_all | solution.py:252
  62.5 0.0 copy-start.7
  62.5 0.0 copy-start.8
  62.5 0.0 copy-done.1
  62.5 0.0 copy-done.2
  62.6 0.0 copy-done.4
  62.6 0.6 copy-done.7
  63.2 0.0 copy-done.8
  63.2 1.2 shard_map.114
  64.4 20.1 %all_to_all.37 = bf16[128,8,128]{2,1,0:T(8,128)(2,1)S(1)} all-to-all(bf16[128,8,128]{2,1,0:T(8,128)(2,1)S(1)} %bitcast.28), channel_id=1, replica_groups=mesh['rh'=8,'core'=2,'col'=16] {'rh','col'}, dimensions={0} | all-to-all | bytes 524288 | tf_op jit(solution)/shard_map/all_to_all | solution.py:267
  84.5 3.5 %collective-permute-start.1 = (bf16[128,8,128]{2,1,0:T(8,128)(2,1)S(1)}, bf16[128,8,128]{2,1,0:T(8,128)(2,1)S(1)}, u32[]{:S(2)}, u32[]{:S(2)}) collective-permute-start(bf16[128,8,128]{2,1,0:T(8,128)(2,1)S(1)} %all_to_all.37), channel_id=1, source_target_pairs={{0,16},{16,0},{1,17},{17,1},{2,18},{18,2},{3,19},{19,3},{4,20},{20... | collective-permute-start | bytes 786440 | tf_op jit(solution)/shard_map/ppermute | solution.py:234
  88.0 1.2 collective-permute-done.1
  89.1 2.4 %shard_map.115 = bf16[8,16,16,128]{3,2,1,0:T(8,128)(2,1)} custom-call(bf16[8,8,16,128]{3,2,1,0:T(8,128)(2,1)S(1)} %bitcast.24, bf16[8,8,16,128]{3,2,1,0:T(8,128)(2,1)S(1)} %bitcast.30, bf16[2,8,2,32,512]{4,3,2,1,0:T(8,128)(2,1)S(1)} %get-tuple-element.17.mats_ref), custom_call_target="tpu_custom_call" | custom-call | tf_op jit(solution)/shard_map/pallas_call | solution.py:269
  91.6 7.2 %all-to-all-start.3 = ((bf16[128,16,128]{2,1,0:T(8,128)(2,1)}), bf16[128,16,128]{2,1,0:T(8,128)(2,1)S(1)}, u32[]{:S(2)}, u32[]{:S(2)}) async-start(bf16[128,16,128]{2,1,0:T(8,128)(2,1)} %bitcast.13), calls=%async_computation.3 | async-start | bytes 1048576 | tf_op jit(solution)/shard_map/all_to_all | solution.py:275
  98.8 16.3 %all-to-all-done.3.grads_ref = bf16[128,16,128]{2,1,0:T(8,128)(2,1)S(1)} async-done(((bf16[128,16,128]{2,1,0:T(8,128)(2,1)}), bf16[128,16,128]{2,1,0:T(8,128)(2,1)S(1)}, u32[]{:S(2)}, u32[]{:S(2)}) %all-to-all-start.3) | async-done | bytes 524320 | tf_op jit(solution)/shard_map/all_to_all | solution.py:275
  115.1 2.6 %shard_map.116 = (bf16[4,8,32,128]{3,2,1,0:T(8,128)(2,1)}, f32[5,128,128]{2,1,0:T(8,128)S(1)}) custom-call(s32[1]{0:T(128)S(6)} %copy.18.valid_ref, bf16[128,16,128]{2,1,0:T(8,128)(2,1)S(1)} %all-to-all-done.3.grads_ref, bf16[128,1024]{1,0:T(8,128)(2,1)S(1)} %get-tuple-element.18.gg_ref, bf16[128,1024]{1,0:T(8,128)(2,1)S(1)} %get-tuple-element.19.xt_ref, ...), custom_call_target="tpu_custom_call" | custom-call | tf_op jit(solution)/shard_map/pallas_call | solution.py:276
  117.7 13.6 %all_to_all.38 = bf16[16,48,128]{2,1,0:T(8,128)(2,1)S(1)} all-to-all(bf16[16,48,128]{2,1,0:T(8,128)(2,1)S(1)} %bitcast.41), channel_id=1, replica_groups=mesh['rh'=8,'core'=2,'col'=16] {'rh','core'}, dimensions={0} | all-to-all | bytes 393216 | tf_op jit(solution)/shard_map/all_to_all | solution.py:227
  131.4 15.1 %all_to_all.39 = bf16[16,48,128]{2,1,0:T(8,128)(2,1)S(1)} all-to-all(bf16[16,48,128]{2,1,0:T(8,128)(2,1)S(1)} %broadcast_in_dim.4), channel_id=1, replica_groups=mesh['rh'=8,'core'=2,'col'=16] {'col'}, dimensions={0} | all-to-all | bytes 393216 | tf_op jit(solution)/shard_map/all_to_all | solution.py:223
  146.5 11.5 %all_to_all.40 = bf16[16,48,128]{2,1,0:T(8,128)(2,1)S(1)} all-to-all(bf16[16,48,128]{2,1,0:T(8,128)(2,1)S(1)} %broadcast_in_dim.5), channel_id=1, replica_groups=mesh['rh'=8,'core'=2,'col'=16] {'rh','core'}, dimensions={0} | all-to-all | bytes 393216 | tf_op jit(solution)/shard_map/all_to_all | solution.py:223
  158.1 0.6 slice.9
  158.7 0.2 copy.16
  158.9 0.9 copy.17
  (9 shorter events, 0.2 us)
Async XLA Ops:
  1.3 0.7 copy-start.5
  1.3 0.7 copy-start.6
  1.9 0.9 copy-start
  2.9 0.9 copy-start.3
  36.9 4.3 %collective-permute-start = (bf16[128,16,128]{2,1,0:T(8,128)(2,1)S(1)}, bf16[128,16,128]{2,1,0:T(8,128)(2,1)S(1)}, u32[]{:S(2)}, u32[]{:S(2)}) collective-permute-start(bf16[128,16,128]{2,1,0:T(8,128)(2,1)S(1)} %all_to_all.35), channel_id=1, source_target_pairs={{0,16},{16,0},{1,17},{17,1},{2,18},{18,2},{3,19},{19,3},{4,20},{20... | collective-permute-start | bytes 1572872 | tf_op jit(solution)/shard_map/ppermute | solution.py:234
  43.0 19.5 %copy-start.1 = (bf16[128,640]{1,0:T(8,128)(2,1)S(1)}, bf16[128,640]{1,0:T(8,128)(2,1)}, u32[]{:S(2)}) copy-start(bf16[128,640]{1,0:T(8,128)(2,1)} %w_ref.5) | copy-start | bytes 491524
  43.0 19.5 %copy-start.2 = (bf16[32,32,128]{2,1,0:T(8,128)(2,1)S(1)}, bf16[32,32,128]{2,1,0:T(8,128)(2,1)}, u32[]{:S(2)}) copy-start(bf16[32,32,128]{2,1,0:T(8,128)(2,1)} %param.10) | copy-start | bytes 786436
  43.0 19.5 %copy-start.4 = (bf16[128,128]{1,0:T(8,128)(2,1)S(1)}, bf16[128,128]{1,0:T(8,128)(2,1)}, u32[]{:S(2)}) copy-start(bf16[128,128]{1,0:T(8,128)(2,1)} %wo_ref.1) | copy-start | bytes 98308
  62.5 0.7 copy-start.7
  62.5 0.7 copy-start.8
  84.5 4.6 %collective-permute-start.1 = (bf16[128,8,128]{2,1,0:T(8,128)(2,1)S(1)}, bf16[128,8,128]{2,1,0:T(8,128)(2,1)S(1)}, u32[]{:S(2)}, u32[]{:S(2)}) collective-permute-start(bf16[128,8,128]{2,1,0:T(8,128)(2,1)S(1)} %all_to_all.37), channel_id=1, source_target_pairs={{0,16},{16,0},{1,17},{17,1},{2,18},{18,2},{3,19},{19,3},{4,20},{20... | collective-permute-start | bytes 786440 | tf_op jit(solution)/shard_map/ppermute | solution.py:234
  91.6 23.5 %all-to-all-start.3 = ((bf16[128,16,128]{2,1,0:T(8,128)(2,1)}), bf16[128,16,128]{2,1,0:T(8,128)(2,1)S(1)}, u32[]{:S(2)}, u32[]{:S(2)}) async-start(bf16[128,16,128]{2,1,0:T(8,128)(2,1)} %bitcast.13), calls=%async_computation.3 | async-start | bytes 1048576 | tf_op jit(solution)/shard_map/all_to_all | solution.py:275

commit v2 on v1

v2 whole, which is shorter than its diff:
```python
import jax
import jax.numpy as jnp
from jax import lax
from jax.experimental import pallas as pl
from jax.experimental.pallas import tpu as pltpu
from jax.sharding import Mesh
from jax.sharding import PartitionSpec as P

EPS = 1e-05
F32 = jnp.float32
BF16 = jnp.bfloat16
ROW = ("yl", "x", "core")
COL = ("z", "yh")
CHIPS = ("x", "yl", "yh", "z")
VMEM = pl.BlockSpec(memory_space=pltpu.VMEM)
SMEM = pl.BlockSpec(memory_space=pltpu.SMEM)
HBM = pl.BlockSpec(memory_space=pltpu.HBM)
ANY = pl.BlockSpec(memory_space=pl.ANY)


def column(ref):
    wide = jnp.broadcast_to(ref[...], (128, 128)).T
    return jnp.concatenate([wide, wide], axis=1)


def dot(a, b, dims):
    return lax.dot_general(a, b, ((dims[:1], dims[1:]), ((), ())), preferred_element_type=F32)


def norm_unit(values):
    mean = jnp.sum(values, axis=0, keepdims=True) * (1.0 / 128)
    centred = values - mean
    var = jnp.sum(centred * centred, axis=0, keepdims=True) * (1.0 / 128)
    rstd = lax.rsqrt(var + EPS)
    return centred * rstd, rstd


def norm_backward(grad, unit, rstd, gain):
    scaled = grad * gain
    first = jnp.sum(scaled, axis=0, keepdims=True) * (1.0 / 128)
    second = jnp.sum(scaled * unit, axis=0, keepdims=True) * (1.0 / 128)
    return rstd * (scaled - first - unit * second)


def pair_mask(valid, n):
    lane = lax.broadcasted_iota(jnp.int32, (1, 256), 1)
    first = 8 * ((lane // 32) % 4) + 2 * n + lane // 128
    row_block = 8 * lax.axis_index("yl") + 2 * lax.axis_index("x") + lax.axis_index("core")
    col_block = 2 * lax.axis_index("z") + lax.axis_index("yh")
    return ((32 * row_block + first < valid) & (32 * col_block + lane % 32 < valid)).astype(F32)


def lanes_of(n):
    return slice(256 * n, 256 * n + 256)


def load_t(ref, n):
    return jnp.concatenate(
        [ref[:, q].reshape(128, 128).astype(F32).T for q in (2 * n, 2 * n + 1)], axis=1
    )


def load_strided(ref, n, first, stride):
    return jnp.concatenate(
        [ref[pl.ds(first + q, 128, stride=stride), :] for q in (2 * n, 2 * n + 1)], axis=1
    )


def store_strided(ref, n, first, stride, values):
    for d in range(2):
        ref[pl.ds(first + 2 * n + d, 128, stride=stride), :] = values[:, 128 * d : 128 * d + 128]


def swap_groups(parts):
    lane = lax.broadcasted_iota(jnp.int32, parts[0].shape, 1)
    low, even = lane < 64, lane % 64 < 32
    mid = [None] * 4
    for f in range(2):
        x, y = parts[f], parts[f + 2]
        mid[f] = jnp.where(low, x, pltpu.roll(y, 64, 1))
        mid[f + 2] = jnp.where(low, pltpu.roll(x, 64, 1), y)
    out = [None] * 4
    for f in (0, 2):
        x, y = mid[f], mid[f + 1]
        out[f] = jnp.where(even, x, pltpu.roll(y, 32, 1))
        out[f + 1] = jnp.where(even, pltpu.roll(x, 96, 1), y)
    return out


def left_right_kernel(
    valid_ref, x_hbm, w_hbm, gain_hbm, bias_hbm, og_hbm, wo_hbm,
    nt_ref, lr_ref, w_ref, og_ref, wo_ref, x_ref, gain_ref, bias_ref, scr, sem,
):
    pairs = (
        (gain_hbm, gain_ref), (bias_hbm, bias_ref), (x_hbm, x_ref), (w_hbm, w_ref),
        (og_hbm, og_ref), (wo_hbm, wo_ref),
    )
    copies = [pltpu.make_async_copy(src, dst, sem.at[i]) for i, (src, dst) in enumerate(pairs)]
    for copy in copies:
        copy.start()
    for copy in copies[:4]:
        copy.wait()
    gain, bias = column(gain_ref), column(bias_ref)
    for n in range(4):
        x = load_t(x_ref, n)
        unit, _ = norm_unit(x)
        normed = (unit * gain + bias).astype(BF16)
        nt_ref[:, lanes_of(n)] = normed
        proj = dot(w_ref[:, :512], normed, (0, 0))
        mask = pair_mask(valid_ref[0], n)
        left = jax.nn.sigmoid(proj[128:256]) * proj[:128] * mask
        right = jax.nn.sigmoid(proj[384:512]) * proj[256:384] * mask
        store_strided(scr, n, 0, 16, left)
        store_strided(scr, n, 8, 16, right)
    lr_ref[...] = scr[...].reshape(128, 16, 128).astype(BF16)
    for copy in copies[4:]:
        copy.wait()


def prepare_kernel(
    valid_ref, nt_ref, og_ref, w_ref, wo_ref, _, coef_ref, back_ref, scaled_ref, gate_ref
):
    for n in range(4):
        lanes = lanes_of(n)
        proj = dot(w_ref[...], nt_ref[:, lanes], (0, 0))
        mask = pair_mask(valid_ref[0], n)
        for side in range(2):
            val = proj[256 * side : 256 * side + 128]
            sig = jax.nn.sigmoid(proj[256 * side + 128 : 256 * side + 256])
            coef_ref[2 * side, :, lanes] = sig * mask
            coef_ref[2 * side + 1, :, lanes] = val * sig * (1.0 - sig) * mask
        gate = jax.nn.sigmoid(proj[512:])
        cotangent = load_t(og_ref, n)
        scaled = (cotangent * gate).astype(BF16)
        scaled_ref[:, lanes] = scaled
        back_ref[:, lanes] = dot(wo_ref[...], scaled, (1, 0))
        gate_ref[:, lanes] = cotangent * gate * (1.0 - gate)


def assemble(parts, store):
    rows = [y.reshape(8, 8, 128) for y in swap_groups(parts)]
    for h in range(2):
        pair = jnp.concatenate([rows[2 * h], rows[2 * h + 1]], axis=1).astype(BF16)
        store(slice(16 * h, 16 * h + 16), pair.reshape(2, 4, 16, 128))


def disassemble(matrix, t):
    parts = [matrix[:, a, :, 128 * t : 128 * t + 128].reshape(64, 128) for a in range(4)]
    return [x.reshape(8, 8, 128) for x in swap_groups(parts)]


def by_yl(ref, f):
    both = ref[f].astype(F32)
    return jnp.concatenate([both[:, 0], both[:, 1]], axis=0)


def assemble_sides(ref, out):
    for t in range(4):
        both = [by_yl(ref, (slice(None), slice(None), f % 2, 2 * t + f // 2)) for f in range(4)]
        for side in range(2):
            parts = [b[:, 8 * side : 8 * side + 8].reshape(64, 128) for b in both]

            def store(rows, values, side=side, t=t):
                out(side, rows, slice(128 * t, 128 * t + 128), values)

            assemble(parts, store)


def triangle_kernel(own_ref, other_ref, _, mats_ref, tri_ref):
    me = lax.axis_index("core")
    for ref, core in ((own_ref, me), (other_ref, 1 - me)):

        def out(side, rows, lanes, values, core=core):
            mats_ref[side, :, :, core, rows, lanes] = values

        assemble_sides(ref, out)
    left = mats_ref[0, :, :, me].reshape(256, 512)
    right = mats_ref[1].reshape(512, 512)
    tri = dot(left, right, (1, 1)).reshape(8, 4, 8, 512)
    for t in range(4):
        cols = disassemble(tri, t)
        for yh in range(2):
            pair = jnp.concatenate([cols[yh], cols[yh + 2]], axis=1).astype(BF16)
            for yl in range(2):
                tri_ref[:, yl, yh, t] = pair[4 * yl : 4 * yl + 4]


def output_kernel(tri_ref, back_ref, gain_ref, bias_ref, tg_ref, tri16_ref, scr):
    gain, bias = column(gain_ref), column(bias_ref)
    scr[...] = tri_ref[...].astype(F32).reshape(1024, 128)
    for n in range(4):
        unit, rstd = norm_unit(load_strided(scr, n, 0, 8))
        tri16_ref[:, lanes_of(n)] = (unit * gain + bias).astype(BF16)
        grad = norm_backward(back_ref[:, lanes_of(n)], unit, rstd, gain)
        store_strided(scr, n, 0, 8, grad)
    tg_ref[...] = scr[...].reshape(64, 16, 128).astype(BF16)


def gate_kernel(tri16_ref, scaled_ref, gate_ref, nt_ref, wo_ref, _, gg_ref, local_ref):
    projected = dot(wo_ref[...], tri16_ref[...], (0, 0))
    gg = (projected * gate_ref[...]).astype(BF16)
    gg_ref[...] = gg
    local_ref[0] = dot(nt_ref[...], gg, (1, 1))
    local_ref[1] = dot(tri16_ref[...], scaled_ref[...], (1, 1))


def assemble_grad(ref, out):
    for t in range(4):
        parts = [None] * 4
        for yh in range(2):
            both = by_yl(ref, (slice(None), slice(None), yh, t))
            parts[yh] = both[:, :8].reshape(64, 128)
            parts[yh + 2] = both[:, 8:].reshape(64, 128)

        def store(rows, values, t=t):
            out[:, :, rows, 128 * t : 128 * t + 128] = values

        assemble(parts, store)


def own_grads_kernel(own_ref, mats_ref, lg_ref, rg_ref, tg, full):
    me = lax.axis_index("core")
    assemble_grad(own_ref, tg)
    grad = tg[...].reshape(256, 512)
    left_grad = dot(grad, mats_ref[1].reshape(512, 512), (1, 0)).reshape(8, 4, 8, 512)
    for t in range(4):
        for f, block in enumerate(disassemble(left_grad, t)):
            lg_ref[t, f] = block
    left = mats_ref[0, :, :, me].reshape(256, 512)
    full[...] = dot(grad, left, (0, 0)).reshape(2, 4, 2, 32, 512)
    rg_ref[...] = full[:, :, me]


def grads_kernel(other_ref, lg_ref, rg_ref, mats_ref, _, out_ref, tg, full):
    me = lax.axis_index("core")
    assemble_grad(other_ref, tg)
    left = mats_ref[0, :, :, 1 - me].reshape(256, 512)
    full[...] = dot(tg[...].reshape(256, 512), left, (0, 0)).reshape(2, 4, 2, 32, 512)
    right_grad = (full[:, :, me] + rg_ref[...]).reshape(8, 4, 8, 512)
    for t in range(4):
        for f, block in enumerate(disassemble(right_grad, t)):
            both = jnp.concatenate([lg_ref[t, f], block], axis=1).astype(BF16)
            for yl in range(2):
                out_ref[:, yl, f % 2, 2 * t + f // 2] = both[4 * yl : 4 * yl + 4]


def weights_kernel(grads_ref, coef_ref, nt_ref, early_ref, pg_ref, local_ref, scr):
    scr[...] = grads_ref[...].astype(F32).reshape(2048, 128)
    total = None
    for n in range(4):
        lanes = lanes_of(n)
        for side in range(2):
            grad = load_strided(scr, n, 8 * side, 16)
            for part in (2 * side, 2 * side + 1):
                pg_ref[128 * part : 128 * part + 128, lanes] = (
                    grad * coef_ref[part, :, lanes]
                ).astype(BF16)
        local = dot(nt_ref[:, lanes], pg_ref[:, lanes], (1, 1))
        total = local if total is None else total + local
    for b in range(4):
        local_ref[128 * b : 128 * b + 128] = total[:, 128 * b : 128 * b + 128].astype(BF16)
    local_ref[512:] = early_ref[...].reshape(256, 128).astype(BF16)


def input_kernel(pg_ref, gg_ref, x_ref, w_ref, gain_ref, gp_ref):
    gain = column(gain_ref)
    for n in range(4):
        lanes = lanes_of(n)
        unit, rstd = norm_unit(load_t(x_ref, n))
        back = dot(w_ref[:, :512], pg_ref[:, lanes], (1, 0))
        back = back + dot(w_ref[:, 512:], gg_ref[:, lanes], (1, 0))
        grad = norm_backward(back, unit, rstd, gain)
        for d in range(2):
            gp_ref[:, 2 * n + d] = (
                grad[:, 128 * d : 128 * d + 128].T.astype(BF16).reshape(4, 32, 128)
            )


def sum_kernel(parts_ref, _, out_ref):
    total = jnp.sum(parts_ref[...].astype(F32), axis=0, keepdims=True).astype(BF16)
    out_ref[...] = jnp.broadcast_to(total, out_ref.shape)


def unpack_kernel(total_ref, in_ref, out_ref):
    for b in range(6):
        block = total_ref[128 * b : 128 * b + 128].astype(F32) * (1.0 / 512)
        if b < 5:
            in_ref[:, 128 * b : 128 * b + 128] = block
        else:
            out_ref[...] = block


def call(kernel, outs, specs, scratch=(), flops=0):
    size = sum(jnp.dtype(d).itemsize * elements(s) for s, d, *_ in outs)
    return pl.pallas_call(
        kernel,
        out_shape=[(where[0] if where else jax.ShapeDtypeStruct)(s, d) for s, d, *where in outs],
        in_specs=specs,
        out_specs=[VMEM] * len(outs),
        scratch_shapes=[pltpu.VMEM(*s) if isinstance(s, tuple) else s for s in scratch],
        compiler_params=pltpu.CompilerParams(vmem_limit_bytes=16 * 1024 * 1024),
        cost_estimate=pl.CostEstimate(flops=flops, bytes_accessed=2 * size, transcendentals=0),
    )


def elements(shape):
    size = 1
    for n in shape:
        size *= n
    return size


def in_hbm(x):
    return pltpu.with_memory_space_constraint(x, pltpu.HBM)


def exchange(x):
    return lax.all_to_all(x, CHIPS, 0, 0, tiled=True)


def other_core(x):
    return lax.ppermute(x, "core", [(0, 1), (1, 0)])


def exchange_16(x, axes):
    return lax.all_to_all(x, axes, 0, 0, tiled=True)


def add(parts, after):
    (out,) = call(sum_kernel, [((16, 48, 128), BF16)], [VMEM, HBM])(parts, in_hbm(after))
    return out


def shards(pair_act, out_grad, valid_count, w_in, w_out, in_gain, in_bias, out_gain, out_bias):
    in_gain, in_bias, out_gain, out_bias = (
        g.reshape(1, 128) for g in (in_gain, in_bias, out_gain, out_bias)
    )
    tall = (128, 1024)
    matrix = (2, 4, 32, 512)
    x = pair_act.reshape(4, 8, 32, 128)
    y = out_grad.reshape(4, 8, 32, 128)
    normed_t, lr, w_near, y_near, w_out_near = call(
        left_right_kernel,
        [
            (tall, BF16),
            ((128, 16, 128), BF16),
            ((128, 640), BF16, pltpu.VMEM),
            ((4, 8, 32, 128), BF16, pltpu.VMEM),
            ((128, 128), BF16, pltpu.VMEM),
        ],
        [SMEM] + [HBM] * 6,
        [
            ((4, 8, 32, 128), BF16),
            ((1, 128), F32),
            ((1, 128), F32),
            ((2048, 128), F32),
            pltpu.SemaphoreType.DMA((6,)),
        ],
        flops=134_000_000,
    )(valid_count, *(in_hbm(v) for v in (x, w_in, in_gain, in_bias, y, w_out)))
    own = exchange(lr).reshape(4, 2, 2, 8, 16, 128)
    other = other_core(own)
    coef, back, scaled, gate = call(
        prepare_kernel,
        [((4,) + tall, F32, pltpu.VMEM), (tall, F32), (tall, BF16), (tall, F32)],
        [SMEM] + [VMEM] * 4 + [ANY],
        flops=200_000_000,
    )(valid_count, normed_t, y_near, w_near, w_out_near, own)
    mats, tri = call(
        triangle_kernel,
        [((2, 2, 4, 2, 32, 512), BF16), ((4, 2, 2, 4, 16, 128), BF16)],
        [VMEM] * 2 + [ANY],
        flops=134_000_000,
    )(own, other, back)
    tri = exchange(tri.reshape(128, 8, 128))
    tri_grad, tri16 = call(
        output_kernel,
        [((64, 16, 128), BF16), (tall, BF16)],
        [VMEM] * 4,
        [((1024, 128), F32)],
    )(tri.reshape(64, 16, 128), back, out_gain, out_bias)
    own = exchange(tri_grad.reshape(128, 8, 128)).reshape(4, 2, 2, 4, 16, 128)
    other = other_core(own)
    gate_grad, early = call(
        gate_kernel,
        [(tall, BF16), ((2, 128, 128), F32)],
        [VMEM] * 5 + [ANY],
        flops=100_000_000,
    )(tri16, scaled, gate, normed_t, w_out, own)
    scratch = [(matrix, BF16), ((2, 4, 2, 32, 512), F32)]
    left_grad, right_grad = call(
        own_grads_kernel,
        [((4, 4, 8, 8, 128), F32), (matrix, F32)],
        [VMEM] * 2,
        scratch,
        flops=268_000_000,
    )(own, mats)
    (grads,) = call(
        grads_kernel,
        [((4, 2, 2, 8, 16, 128), BF16)],
        [VMEM] * 4 + [ANY],
        scratch,
        flops=134_000_000,
    )(other, left_grad, right_grad, mats, gate_grad)
    grads = exchange(grads.reshape(128, 16, 128))
    proj_grad, local = call(
        weights_kernel,
        [((512, 1024), BF16), ((768, 128), BF16)],
        [VMEM] * 4,
        [((2048, 128), F32)],
        flops=134_000_000,
    )(grads, coef, normed_t, early)
    parts = exchange_16(local.reshape(16, 48, 128), ROW)
    (grad_pair,) = call(
        input_kernel, [((4, 8, 32, 128), BF16, pltpu.HBM)], [VMEM] * 5, flops=168_000_000
    )(proj_grad, gate_grad, x, w_in, in_gain)
    parts = exchange_16(add(parts, grad_pair), ("yh", "z"))
    parts = exchange_16(add(parts, grad_pair), ROW)
    grad_in, grad_out = call(
        unpack_kernel, [((128, 640), F32), ((128, 128), F32)], [VMEM]
    )(parts.reshape(768, 128))
    return grad_pair.reshape(32, 32, 128), grad_in, grad_out


def solution(mesh):
    fine = Mesh(mesh.devices.reshape(2, 4, 2, 8, 2), ("yl", "x", "core", "z", "yh"))
    pairs = P(ROW, COL, None)
    return jax.shard_map(
        shards,
        mesh=fine,
        in_specs=(pairs, pairs, P(), P(), P(), P(), P(), P(), P()),
        out_specs=(pairs, P(), P()),
        check_vma=False,
    )
```

time: 160 us -> 152 us (0.950)
  waiting for transfers between devices: 19 us -> 5.48 us
  blocking collectives: 112 us -> 123 us
  local copies, waits for them, and re-layouts: 4.96 us -> 0.04 us
  starting transfers between devices: 13.4 us -> 10.2 us
  Pallas kernels: 8.88 us -> 12 us
    all_to_all x1, waiting for transfers between devices: 16.3 us -> 5.42 us  [exchange_16(): return lax.all_to_all(x, axes, 0, 0, tiled=True)]
    all_to_all x6, blocking collectives: 112 us -> 123 us  [the longest x4 99.7 us: exchange(): return lax.all_to_all(x, CHIPS, 0, 0, tiled=True)]
    unnamed x19 -> x12, local copies, waits for them, and re-layouts: 4.09 us -> 0.04 us
    pallas_call x5 -> x12, Pallas kernels: 8.88 us -> 12 us  [the longest x1 2.17 us: shards(): call(triangle_kernel, [((2, 2, 4, 2, 32, 512), BF16), ((4, 2, 2, 4, 16, 1...]
    ppermute x2, waiting for transfers between devices: 2.7 us -> 0.06 us  [other_core(): return lax.ppermute(x, 'core', [(0, 1), (1, 0)])]
    all_to_all x1, starting transfers between devices: 7.18 us -> 4.81 us  [exchange_16(): return lax.all_to_all(x, axes, 0, 0, tiled=True)]
  transfers between devices with their start and end apart: 3 -> 3, of which waited for: 3 -> 2; matrix products, arithmetic and copies ran while one was open for 0% -> 0% of each run, Pallas kernels for 0% -> 3%
where the time goes in v2:
time: 152 us
  blocking collectives  123 us (81%)
  Pallas kernels  12 us (8%)
  starting transfers between devices  10.2 us (7%)
  waiting for transfers between devices  5.48 us (4%)
    all_to_all x4, blocking collectives, exchange(): return lax.all_to_all(x, CHIPS, 0, 0, tiled=True)  99.7 us
    all_to_all x2, blocking collectives, exchange_16(): return lax.all_to_all(x, axes, 0, 0, tiled=True)  23 us
    ppermute x2, starting transfers between devices, other_core(): return lax.ppermute(x, 'core', [(0, 1), (1, 0)])  5.42 us
    all_to_all x1, waiting for transfers between devices, exchange_16(): return lax.all_to_all(x, axes, 0, 0, tiled=True)  5.42 us
    all_to_all x1, starting transfers between devices, exchange_16(): return lax.all_to_all(x, axes, 0, 0, tiled=True)  4.81 us
  transfers between devices with their start and end apart: 3, of which 2 were waited for; matrix products, arithmetic and copies ran while one was open for 0% of the time, Pallas kernels for 3%

profile of v2, /device:TPU:1, one launch (start us, length us, event | category | flops | bytes accessed | tf_op | source)
XLA Modules:
  0.0 151.9 jit_solution(5212545691319184300)
XLA Ops:
  1.3 1.9 %shard_map.112 = (bf16[128,1024]{1,0:T(8,128)(2,1)S(1)}, bf16[128,16,128]{2,1,0:T(8,128)(2,1)S(1)}, bf16[128,640]{1,0:T(8,128)(2,1)S(1)}, bf16[4,8,32,128]{3,2,1,0:T(8,128)(2,1)S(1)}, bf16[128,128]{1,0:T(8,128)(2,1)S(1)}) custom-call(s32[1]{0:T(128)S(6)} %copy.12.valid_ref, bf16[4,8,32,128]{3,2,1,0:T(8,128)(2,1)} %bitcast.22, bf16[128,640]{1,0:T(8,128)(2,1)} %w_ref.1, ...), custom_call_target="tpu_custom_call" | custom-call | flops 134000000 | bytes 2490368 | tf_op jit(solution)/shard_map/pallas_call | solution.py:342
  3.2 0.0 copy-start.4
  3.2 0.0 copy-start.5
  3.2 35.4 %all_to_all.35 = bf16[128,16,128]{2,1,0:T(8,128)(2,1)S(1)} all-to-all(bf16[128,16,128]{2,1,0:T(8,128)(2,1)S(1)} %get-tuple-element.24), channel_id=1, replica_groups=mesh['yl'=2,'x'=4,'core'=2,'z'=8,'yh'=2] {'x','yl','yh','z'}, dimensions={0} | all-to-all | bytes 1048576 | tf_op jit(solution)/shard_map/all_to_all | solution.py:318
  38.6 2.4 %collective-permute-start = (bf16[4,2,2,8,16,128]{5,4,3,2,1,0:T(8,128)(2,1)S(1)}, bf16[4,2,2,8,16,128]{5,4,3,2,1,0:T(8,128)(2,1)S(1)}, u32[]{:S(2)}, u32[]{:S(2)}) collective-permute-start(bf16[4,2,2,8,16,128]{5,4,3,2,1,0:T(8,128)(2,1)S(1)} %bitcast.15), channel_id=1, source_target_pairs={{0,16},{16,0},{1,17},{17,1},{2,18},{18,2},{3,19},{19,3},{4,20},{20... | collective-permute-start | bytes 1572872 | tf_op jit(solution)/shard_map/ppermute | solution.py:322
  41.0 0.0 copy-start.2
  41.0 1.5 shard_map.113
  42.5 0.1 collective-permute-done.other_ref
  42.5 2.2 %shard_map.114 = (bf16[2,2,4,2,32,512]{5,4,3,2,1,0:T(8,128)(2,1)S(1)}, bf16[4,2,2,4,16,128]{5,4,3,2,1,0:T(8,128)(2,1)S(1)}) custom-call(bf16[4,2,2,8,16,128]{5,4,3,2,1,0:T(8,128)(2,1)S(1)} %bitcast.17, bf16[4,2,2,8,16,128]{5,4,3,2,1,0:T(8,128)(2,1)S(1)} %collective-permute-done.other_ref, f32[128,1024]{1,0:T(8,128)S(1)} %get-tuple-element.29._.back_ref), custom_call_target="tpu_custom_call" | custom-call | flops 134000000 | bytes 2621440 | tf_op jit(solution)/shard_map/pallas_call | solution.py:369
  44.7 20.0 %all_to_all.36 = bf16[128,8,128]{2,1,0:T(8,128)(2,1)S(1)} all-to-all(bf16[128,8,128]{2,1,0:T(8,128)(2,1)S(1)} %bitcast.26), channel_id=1, replica_groups=mesh['yl'=2,'x'=4,'core'=2,'z'=8,'yh'=2] {'x','yl','yh','z'}, dimensions={0} | all-to-all | bytes 524288 | tf_op jit(solution)/shard_map/all_to_all | solution.py:318
  64.8 0.0 copy-done.4
  64.8 0.0 copy-done.5
  64.8 0.5 shard_map.115
  65.3 18.5 %all_to_all.37 = bf16[128,8,128]{2,1,0:T(8,128)(2,1)S(1)} all-to-all(bf16[128,8,128]{2,1,0:T(8,128)(2,1)S(1)} %bitcast.27), channel_id=1, replica_groups=mesh['yl'=2,'x'=4,'core'=2,'z'=8,'yh'=2] {'x','yl','yh','z'}, dimensions={0} | all-to-all | bytes 524288 | tf_op jit(solution)/shard_map/all_to_all | solution.py:318
  83.8 3.0 %collective-permute-start.1 = (bf16[4,2,2,4,16,128]{5,4,3,2,1,0:T(8,128)(2,1)S(1)}, bf16[4,2,2,4,16,128]{5,4,3,2,1,0:T(8,128)(2,1)S(1)}, u32[]{:S(2)}, u32[]{:S(2)}) collective-permute-start(bf16[4,2,2,4,16,128]{5,4,3,2,1,0:T(8,128)(2,1)S(1)} %bitcast.18), channel_id=1, source_target_pairs={{0,16},{16,0},{1,17},{17,1},{2,18},{18,2},{3,19},{19,3},{4,20},{20... | collective-permute-start | bytes 786440 | tf_op jit(solution)/shard_map/ppermute | solution.py:322
  86.8 0.0 copy-done.2
  86.8 0.5 shard_map.117
  87.3 1.0 shard_map.116
  88.3 0.0 collective-permute-done.1.other_ref
  88.3 0.9 shard_map.118
  89.2 0.0 copy-start
  89.3 0.0 copy-start.1
  89.3 0.0 copy-start.3
  89.3 25.8 %all_to_all.38.grads_ref = bf16[128,16,128]{2,1,0:T(8,128)(2,1)S(1)} all-to-all(bf16[128,16,128]{2,1,0:T(8,128)(2,1)S(1)} %bitcast.21), channel_id=1, replica_groups=mesh['yl'=2,'x'=4,'core'=2,'z'=8,'yh'=2] {'x','yl','yh','z'}, dimensions={0} | all-to-all | bytes 1048576 | tf_op jit(solution)/shard_map/all_to_all | solution.py:318
  115.1 1.4 shard_map.119
  116.5 4.8 %all-to-all-start.4 = ((bf16[16,48,128]{2,1,0:T(8,128)(2,1)}), bf16[16,48,128]{2,1,0:T(8,128)(2,1)S(1)}, u32[]{:S(2)}, u32[]{:S(2)}) async-start(bf16[16,48,128]{2,1,0:T(8,128)(2,1)} %bitcast.13), calls=%async_computation.4 | async-start | bytes 393216 | tf_op jit(solution)/shard_map/all_to_all | solution.py:326
  121.3 0.0 copy-done
  121.3 0.0 copy-done.1
  121.3 0.0 copy-done.3
  121.3 1.3 shard_map.120._
  122.6 5.4 %all-to-all-done.4.parts_ref = bf16[16,48,128]{2,1,0:T(8,128)(2,1)S(1)} async-done(((bf16[16,48,128]{2,1,0:T(8,128)(2,1)}), bf16[16,48,128]{2,1,0:T(8,128)(2,1)S(1)}, u32[]{:S(2)}, u32[]{:S(2)}) %all-to-all-start.4) | async-done | bytes 196640 | tf_op jit(solution)/shard_map/all_to_all | solution.py:326
  128.1 11.6 %all_to_all.39.parts_ref = bf16[16,48,128]{2,1,0:T(8,128)(2,1)S(1)} all-to-all(bf16[16,48,128]{2,1,0:T(8,128)(2,1)S(1)} %shard_map.121), channel_id=1, replica_groups=mesh['yl'=2,'x'=4,'core'=2,'z'=8,'yh'=2] {'yh','z'}, dimensions={0} | all-to-all | bytes 393216 | tf_op jit(solution)/shard_map/all_to_all | solution.py:326
  139.7 11.4 %all_to_all.40 = bf16[16,48,128]{2,1,0:T(8,128)(2,1)S(1)} all-to-all(bf16[16,48,128]{2,1,0:T(8,128)(2,1)S(1)} %shard_map.122), channel_id=1, replica_groups=mesh['yl'=2,'x'=4,'core'=2,'z'=8,'yh'=2] {'yl','x','core'}, dimensions={0} | all-to-all | bytes 393216 | tf_op jit(solution)/shard_map/all_to_all | solution.py:326
  151.1 0.8 shard_map.123
  (2 shorter events, 0.1 us)
Async XLA Ops:
  3.2 61.6 %copy-start.4 = (f32[128]{0:T(128)S(1)}, f32[128]{0:T(128)}, u32[]{:S(2)}) copy-start(f32[128]{0:T(128)} %param.16) | copy-start | bytes 1540
  3.2 61.6 %copy-start.5 = (f32[128]{0:T(128)S(1)}, f32[128]{0:T(128)}, u32[]{:S(2)}) copy-start(f32[128]{0:T(128)} %param.17) | copy-start | bytes 1540
  38.6 3.9 %collective-permute-start = (bf16[4,2,2,8,16,128]{5,4,3,2,1,0:T(8,128)(2,1)S(1)}, bf16[4,2,2,8,16,128]{5,4,3,2,1,0:T(8,128)(2,1)S(1)}, u32[]{:S(2)}, u32[]{:S(2)}) collective-permute-start(bf16[4,2,2,8,16,128]{5,4,3,2,1,0:T(8,128)(2,1)S(1)} %bitcast.15), channel_id=1, source_target_pairs={{0,16},{16,0},{1,17},{17,1},{2,18},{18,2},{3,19},{19,3},{4,20},{20... | collective-permute-start | bytes 1572872 | tf_op jit(solution)/shard_map/ppermute | solution.py:322
  41.0 45.8 %copy-start.2 = (bf16[128,128]{1,0:T(8,128)(2,1)S(1)}, bf16[128,128]{1,0:T(8,128)(2,1)}, u32[]{:S(2)}) copy-start(bf16[128,128]{1,0:T(8,128)(2,1)} %wo_ref.1) | copy-start | bytes 98308
  83.8 4.5 %collective-permute-start.1 = (bf16[4,2,2,4,16,128]{5,4,3,2,1,0:T(8,128)(2,1)S(1)}, bf16[4,2,2,4,16,128]{5,4,3,2,1,0:T(8,128)(2,1)S(1)}, u32[]{:S(2)}, u32[]{:S(2)}) collective-permute-start(bf16[4,2,2,4,16,128]{5,4,3,2,1,0:T(8,128)(2,1)S(1)} %bitcast.18), channel_id=1, source_target_pairs={{0,16},{16,0},{1,17},{17,1},{2,18},{18,2},{3,19},{19,3},{4,20},{20... | collective-permute-start | bytes 786440 | tf_op jit(solution)/shard_map/ppermute | solution.py:322
  89.2 32.1 %copy-start = (bf16[32,32,128]{2,1,0:T(8,128)(2,1)S(1)}, bf16[32,32,128]{2,1,0:T(8,128)(2,1)}, u32[]{:S(2)}) copy-start(bf16[32,32,128]{2,1,0:T(8,128)(2,1)} %param.9) | copy-start | bytes 786436
  89.3 32.1 %copy-start.1 = (bf16[128,640]{1,0:T(8,128)(2,1)S(1)}, bf16[128,640]{1,0:T(8,128)(2,1)}, u32[]{:S(2)}) copy-start(bf16[128,640]{1,0:T(8,128)(2,1)} %w_ref.1) | copy-start | bytes 491524
  89.3 32.1 %copy-start.3 = (f32[128]{0:T(128)S(1)}, f32[128]{0:T(128)}, u32[]{:S(2)}) copy-start(f32[128]{0:T(128)} %param.14) | copy-start | bytes 1540
  116.5 11.5 %all-to-all-start.4 = ((bf16[16,48,128]{2,1,0:T(8,128)(2,1)}), bf16[16,48,128]{2,1,0:T(8,128)(2,1)S(1)}, u32[]{:S(2)}, u32[]{:S(2)}) async-start(bf16[16,48,128]{2,1,0:T(8,128)(2,1)} %bitcast.13), calls=%async_computation.4 | async-start | bytes 393216 | tf_op jit(solution)/shard_map/all_to_all | solution.py:326

commit v3 on v2

--- a/solution.py
+++ b/solution.py
@@ -13,7 +13,6 @@
 COL = ("z", "yh")
 CHIPS = ("x", "yl", "yh", "z")
 VMEM = pl.BlockSpec(memory_space=pltpu.VMEM)
-SMEM = pl.BlockSpec(memory_space=pltpu.SMEM)
 HBM = pl.BlockSpec(memory_space=pltpu.HBM)
 ANY = pl.BlockSpec(memory_space=pl.ANY)
 
@@ -47,6 +46,7 @@
     first = 8 * ((lane // 32) % 4) + 2 * n + lane // 128
     row_block = 8 * lax.axis_index("yl") + 2 * lax.axis_index("x") + lax.axis_index("core")
     col_block = 2 * lax.axis_index("z") + lax.axis_index("yh")
+    valid = jnp.broadcast_to(valid, (1, 256))
     return ((32 * row_block + first < valid) & (32 * col_block + lane % 32 < valid)).astype(F32)
 
 
@@ -71,35 +71,46 @@
         ref[pl.ds(first + 2 * n + d, 128, stride=stride), :] = values[:, 128 * d : 128 * d + 128]
 
 
-def swap_groups(parts):
-    lane = lax.broadcasted_iota(jnp.int32, parts[0].shape, 1)
-    low, even = lane < 64, lane % 64 < 32
-    mid = [None] * 4
-    for f in range(2):
-        x, y = parts[f], parts[f + 2]
-        mid[f] = jnp.where(low, x, pltpu.roll(y, 64, 1))
-        mid[f + 2] = jnp.where(low, pltpu.roll(x, 64, 1), y)
-    out = [None] * 4
-    for f in (0, 2):
-        x, y = mid[f], mid[f + 1]
-        out[f] = jnp.where(even, x, pltpu.roll(y, 32, 1))
-        out[f + 1] = jnp.where(even, pltpu.roll(x, 96, 1), y)
-    return out
+def swap_lanes(x, y, width):
+    shape = x.shape
+    x, y = x.reshape(128, 128), y.reshape(128, 128)
+    first = lax.broadcasted_iota(jnp.int32, (128, 128), 1) % (2 * width) < width
+    left = jnp.where(first, x, pltpu.roll(y, width, 1))
+    right = jnp.where(first, pltpu.roll(x, 128 - width, 1), y)
+    return left.reshape(shape), right.reshape(shape)
+
+
+def swap_rows(x, y):
+    return (
+        jnp.concatenate([x[:, :8], y[:, :8]], axis=1),
+        jnp.concatenate([x[:, 8:], y[:, 8:]], axis=1),
+    )
+
+
+def to_rows(x, y):
+    return swap_lanes(*swap_rows(*swap_lanes(x, y, 32)), 64)
+
+
+def to_blocks(x, y):
+    return swap_lanes(*swap_rows(*swap_lanes(x, y, 64)), 32)
 
 
 def left_right_kernel(
-    valid_ref, x_hbm, w_hbm, gain_hbm, bias_hbm, og_hbm, wo_hbm,
-    nt_ref, lr_ref, w_ref, og_ref, wo_ref, x_ref, gain_ref, bias_ref, scr, sem,
+    x_hbm, w_hbm, gain_hbm, bias_hbm, og_hbm, wo_hbm,
+    nt_ref, lr_ref, w_ref, og_ref, wo_ref,
+    x_ref, gain_ref, bias_ref, scr, sem,
 ):
     pairs = (
-        (gain_hbm, gain_ref), (bias_hbm, bias_ref), (x_hbm, x_ref), (w_hbm, w_ref),
+        (x_hbm, x_ref), (w_hbm, w_ref), (gain_hbm, gain_ref), (bias_hbm, bias_ref),
         (og_hbm, og_ref), (wo_hbm, wo_ref),
     )
     copies = [pltpu.make_async_copy(src, dst, sem.at[i]) for i, (src, dst) in enumerate(pairs)]
-    for copy in copies:
+    for copy in copies[:4]:
         copy.start()
     for copy in copies[:4]:
         copy.wait()
+    for copy in copies[4:]:
+        copy.start()
     gain, bias = column(gain_ref), column(bias_ref)
     for n in range(4):
         x = load_t(x_ref, n)
@@ -107,9 +118,8 @@
         normed = (unit * gain + bias).astype(BF16)
         nt_ref[:, lanes_of(n)] = normed
         proj = dot(w_ref[:, :512], normed, (0, 0))
-        mask = pair_mask(valid_ref[0], n)
-        left = jax.nn.sigmoid(proj[128:256]) * proj[:128] * mask
-        right = jax.nn.sigmoid(proj[384:512]) * proj[256:384] * mask
+        left = jax.nn.sigmoid(proj[128:256]) * proj[:128]
+        right = jax.nn.sigmoid(proj[384:512]) * proj[256:384]
         store_strided(scr, n, 0, 16, left)
         store_strided(scr, n, 8, 16, right)
     lr_ref[...] = scr[...].reshape(128, 16, 128).astype(BF16)
@@ -123,7 +133,7 @@
     for n in range(4):
         lanes = lanes_of(n)
         proj = dot(w_ref[...], nt_ref[:, lanes], (0, 0))
-        mask = pair_mask(valid_ref[0], n)
+        mask = pair_mask(valid_ref[...], n)
         for side in range(2):
             val = proj[256 * side : 256 * side + 128]
             sig = jax.nn.sigmoid(proj[256 * side + 128 : 256 * side + 256])
@@ -137,52 +147,40 @@
         gate_ref[:, lanes] = cotangent * gate * (1.0 - gate)
 
 
-def assemble(parts, store):
-    rows = [y.reshape(8, 8, 128) for y in swap_groups(parts)]
-    for h in range(2):
-        pair = jnp.concatenate([rows[2 * h], rows[2 * h + 1]], axis=1).astype(BF16)
-        store(slice(16 * h, 16 * h + 16), pair.reshape(2, 4, 16, 128))
-
-
-def disassemble(matrix, t):
-    parts = [matrix[:, a, :, 128 * t : 128 * t + 128].reshape(64, 128) for a in range(4)]
-    return [x.reshape(8, 8, 128) for x in swap_groups(parts)]
-
-
-def by_yl(ref, f):
-    both = ref[f].astype(F32)
-    return jnp.concatenate([both[:, 0], both[:, 1]], axis=0)
-
-
-def assemble_sides(ref, out):
-    for t in range(4):
-        both = [by_yl(ref, (slice(None), slice(None), f % 2, 2 * t + f // 2)) for f in range(4)]
-        for side in range(2):
-            parts = [b[:, 8 * side : 8 * side + 8].reshape(64, 128) for b in both]
-
-            def store(rows, values, side=side, t=t):
-                out(side, rows, slice(128 * t, 128 * t + 128), values)
-
-            assemble(parts, store)
-
-
-def triangle_kernel(own_ref, other_ref, _, mats_ref, tri_ref):
+def lanes_t(t):
+    return slice(128 * t, 128 * t + 128)
+
+
+def by_yl(ref, yh, z):
+    return jnp.concatenate([ref[:, 0, yh, z], ref[:, 1, yh, z]], axis=0)
+
+
+def matrix_blocks(matrix, t):
+    return to_blocks(matrix[:, :16, lanes_t(t)], matrix[:, 16:, lanes_t(t)])
+
+
+def triangle_kernel(valid_ref, own_ref, other_ref, _, mats_ref, tri_ref):
     me = lax.axis_index("core")
+    dims = (8, 16, 128)
+    valid = jnp.broadcast_to(valid_ref[...].reshape(1, 1, 1), dims)
+    block, row, lane = (lax.broadcasted_iota(jnp.int32, dims, d) for d in range(3))
     for ref, core in ((own_ref, me), (other_ref, 1 - me)):
-
-        def out(side, rows, lanes, values, core=core):
-            mats_ref[side, :, :, core, rows, lanes] = values
-
-        assemble_sides(ref, out)
+        token = 64 * block + row + 32 * core
+        for t in range(4):
+            sides = [swap_rows(by_yl(ref, yh, 2 * t), by_yl(ref, yh, 2 * t + 1)) for yh in range(2)]
+            for side in range(2):
+                for h, values in enumerate(to_rows(sides[0][side], sides[1][side])):
+                    keep = (token + 16 * h < valid) & (lane + 128 * t < valid)
+                    mats_ref[side, :, :, core, 16 * h : 16 * h + 16, lanes_t(t)] = jnp.where(
+                        keep, values, jnp.zeros_like(values)
+                    ).reshape(2, 4, 16, 128)
     left = mats_ref[0, :, :, me].reshape(256, 512)
     right = mats_ref[1].reshape(512, 512)
-    tri = dot(left, right, (1, 1)).reshape(8, 4, 8, 512)
+    tri = dot(left, right, (1, 1)).astype(BF16).reshape(8, 32, 512)
     for t in range(4):
-        cols = disassemble(tri, t)
-        for yh in range(2):
-            pair = jnp.concatenate([cols[yh], cols[yh + 2]], axis=1).astype(BF16)
+        for yh, block in enumerate(matrix_blocks(tri, t)):
             for yl in range(2):
-                tri_ref[:, yl, yh, t] = pair[4 * yl : 4 * yl + 4]
+                tri_ref[:, yl, yh, t] = block[4 * yl : 4 * yl + 4]
 
 
 def output_kernel(tri_ref, back_ref, gain_ref, bias_ref, tg_ref, tri16_ref, scr):
@@ -206,26 +204,18 @@
 
 def assemble_grad(ref, out):
     for t in range(4):
-        parts = [None] * 4
-        for yh in range(2):
-            both = by_yl(ref, (slice(None), slice(None), yh, t))
-            parts[yh] = both[:, :8].reshape(64, 128)
-            parts[yh + 2] = both[:, 8:].reshape(64, 128)
-
-        def store(rows, values, t=t):
-            out[:, :, rows, 128 * t : 128 * t + 128] = values
-
-        assemble(parts, store)
+        for h, values in enumerate(to_rows(by_yl(ref, 0, t), by_yl(ref, 1, t))):
+            out[:, :, 16 * h : 16 * h + 16, lanes_t(t)] = values.reshape(2, 4, 16, 128)
 
 
 def own_grads_kernel(own_ref, mats_ref, lg_ref, rg_ref, tg, full):
     me = lax.axis_index("core")
     assemble_grad(own_ref, tg)
     grad = tg[...].reshape(256, 512)
-    left_grad = dot(grad, mats_ref[1].reshape(512, 512), (1, 0)).reshape(8, 4, 8, 512)
+    left_grad = dot(grad, mats_ref[1].reshape(512, 512), (1, 0)).astype(BF16).reshape(8, 32, 512)
     for t in range(4):
-        for f, block in enumerate(disassemble(left_grad, t)):
-            lg_ref[t, f] = block
+        for yh, block in enumerate(matrix_blocks(left_grad, t)):
+            lg_ref[t, yh] = block
     left = mats_ref[0, :, :, me].reshape(256, 512)
     full[...] = dot(grad, left, (0, 0)).reshape(2, 4, 2, 32, 512)
     rg_ref[...] = full[:, :, me]
@@ -236,38 +226,41 @@
     assemble_grad(other_ref, tg)
     left = mats_ref[0, :, :, 1 - me].reshape(256, 512)
     full[...] = dot(tg[...].reshape(256, 512), left, (0, 0)).reshape(2, 4, 2, 32, 512)
-    right_grad = (full[:, :, me] + rg_ref[...]).reshape(8, 4, 8, 512)
+    right_grad = (full[:, :, me] + rg_ref[...]).astype(BF16).reshape(8, 32, 512)
     for t in range(4):
-        for f, block in enumerate(disassemble(right_grad, t)):
-            both = jnp.concatenate([lg_ref[t, f], block], axis=1).astype(BF16)
-            for yl in range(2):
-                out_ref[:, yl, f % 2, 2 * t + f // 2] = both[4 * yl : 4 * yl + 4]
-
-
-def weights_kernel(grads_ref, coef_ref, nt_ref, early_ref, pg_ref, local_ref, scr):
+        for yh, block in enumerate(matrix_blocks(right_grad, t)):
+            for z, both in enumerate(swap_rows(lg_ref[t, yh], block)):
+                for yl in range(2):
+                    out_ref[:, yl, yh, 2 * t + z] = both[4 * yl : 4 * yl + 4]
+
+
+def proj_grad(scr, coef_ref, n):
+    parts = []
+    for side in range(2):
+        grad = load_strided(scr, n, 8 * side, 16)
+        for part in (2 * side, 2 * side + 1):
+            parts.append((grad * coef_ref[part, :, lanes_of(n)]).astype(BF16))
+    return jnp.concatenate(parts, axis=0)
+
+
+def weights_kernel(grads_ref, coef_ref, nt_ref, early_ref, local_ref, scr):
     scr[...] = grads_ref[...].astype(F32).reshape(2048, 128)
     total = None
     for n in range(4):
-        lanes = lanes_of(n)
-        for side in range(2):
-            grad = load_strided(scr, n, 8 * side, 16)
-            for part in (2 * side, 2 * side + 1):
-                pg_ref[128 * part : 128 * part + 128, lanes] = (
-                    grad * coef_ref[part, :, lanes]
-                ).astype(BF16)
-        local = dot(nt_ref[:, lanes], pg_ref[:, lanes], (1, 1))
+        local = dot(nt_ref[:, lanes_of(n)], proj_grad(scr, coef_ref, n), (1, 1))
         total = local if total is None else total + local
     for b in range(4):
         local_ref[128 * b : 128 * b + 128] = total[:, 128 * b : 128 * b + 128].astype(BF16)
     local_ref[512:] = early_ref[...].reshape(256, 128).astype(BF16)
 
 
-def input_kernel(pg_ref, gg_ref, x_ref, w_ref, gain_ref, gp_ref):
+def input_kernel(grads_ref, coef_ref, gg_ref, x_ref, w_ref, gain_ref, gp_ref, scr):
+    scr[...] = grads_ref[...].astype(F32).reshape(2048, 128)
     gain = column(gain_ref)
     for n in range(4):
         lanes = lanes_of(n)
         unit, rstd = norm_unit(load_t(x_ref, n))
-        back = dot(w_ref[:, :512], pg_ref[:, lanes], (1, 0))
+        back = dot(w_ref[:, :512], proj_grad(scr, coef_ref, n), (1, 0))
         back = back + dot(w_ref[:, 512:], gg_ref[:, lanes], (1, 0))
         grad = norm_backward(back, unit, rstd, gain)
         for d in range(2):
@@ -337,6 +330,7 @@
     )
     tall = (128, 1024)
     matrix = (2, 4, 32, 512)
+    valid = valid_count.reshape(1, 1)
     x = pair_act.reshape(4, 8, 32, 128)
     y = out_grad.reshape(4, 8, 32, 128)
     normed_t, lr, w_near, y_near, w_out_near = call(
@@ -348,7 +342,7 @@
             ((4, 8, 32, 128), BF16, pltpu.VMEM),
             ((128, 128), BF16, pltpu.VMEM),
         ],
-        [SMEM] + [HBM] * 6,
+        [HBM] * 6,
         [
             ((4, 8, 32, 128), BF16),
             ((1, 128), F32),
@@ -357,21 +351,21 @@
             pltpu.SemaphoreType.DMA((6,)),
         ],
         flops=134_000_000,
-    )(valid_count, *(in_hbm(v) for v in (x, w_in, in_gain, in_bias, y, w_out)))
+    )(*(in_hbm(v) for v in (x, w_in, in_gain, in_bias, y, w_out)))
     own = exchange(lr).reshape(4, 2, 2, 8, 16, 128)
     other = other_core(own)
     coef, back, scaled, gate = call(
         prepare_kernel,
         [((4,) + tall, F32, pltpu.VMEM), (tall, F32), (tall, BF16), (tall, F32)],
-        [SMEM] + [VMEM] * 4 + [ANY],
+        [VMEM] * 5 + [ANY],
         flops=200_000_000,
-    )(valid_count, normed_t, y_near, w_near, w_out_near, own)
+    )(valid, normed_t, y_near, w_near, w_out_near, own)
     mats, tri = call(
         triangle_kernel,
         [((2, 2, 4, 2, 32, 512), BF16), ((4, 2, 2, 4, 16, 128), BF16)],
-        [VMEM] * 2 + [ANY],
+        [VMEM] * 3 + [ANY],
         flops=134_000_000,
-    )(own, other, back)
+    )(valid, own, other, back)
     tri = exchange(tri.reshape(128, 8, 128))
     tri_grad, tri16 = call(
         output_kernel,
@@ -390,7 +384,7 @@
     scratch = [(matrix, BF16), ((2, 4, 2, 32, 512), F32)]
     left_grad, right_grad = call(
         own_grads_kernel,
-        [((4, 4, 8, 8, 128), F32), (matrix, F32)],
+        [((4, 2, 8, 16, 128), BF16), (matrix, F32)],
         [VMEM] * 2,
         scratch,
         flops=268_000_000,
@@ -403,17 +397,21 @@
         flops=134_000_000,
     )(other, left_grad, right_grad, mats, gate_grad)
     grads = exchange(grads.reshape(128, 16, 128))
-    proj_grad, local = call(
+    (local,) = call(
         weights_kernel,
-        [((512, 1024), BF16), ((768, 128), BF16)],
+        [((768, 128), BF16)],
         [VMEM] * 4,
         [((2048, 128), F32)],
         flops=134_000_000,
     )(grads, coef, normed_t, early)
     parts = exchange_16(local.reshape(16, 48, 128), ROW)
     (grad_pair,) = call(
-        input_kernel, [((4, 8, 32, 128), BF16, pltpu.HBM)], [VMEM] * 5, flops=168_000_000
-    )(proj_grad, gate_grad, x, w_in, in_gain)
+        input_kernel,
+        [((4, 8, 32, 128), BF16, pltpu.HBM)],
+        [VMEM] * 6,
+        [((2048, 128), F32)],
+        flops=168_000_000,
+    )(grads, coef, gate_grad, x, w_in, in_gain)
     parts = exchange_16(add(parts, grad_pair), ("yh", "z"))
     parts = exchange_16(add(parts, grad_pair), ROW)
     grad_in, grad_out = call(

time: 152 us -> 152 us (level)
  transfers between devices with their start and end apart: 3 -> 3, of which waited for: 2 -> 1; matrix products, arithmetic and copies ran while one was open for 0% -> 0% of each run, Pallas kernels for 3% -> 3%
where the time goes in v3:
time: 152 us; the launch traced here: 151 us
  blocking collectives  123 us (81%)
  Pallas kernels  11.7 us (8%)
  starting transfers between devices  10.1 us (7%)
  waiting for transfers between devices  5.03 us (3%)
    all_to_all x4, blocking collectives, exchange(): return lax.all_to_all(x, CHIPS, 0, 0, tiled=True)  100 us
    all_to_all x2, blocking collectives, exchange_16(): return lax.all_to_all(x, axes, 0, 0, tiled=True)  23 us
    all_to_all x1, starting transfers between devices, exchange_16(): return lax.all_to_all(x, axes, 0, 0, tiled=True)  5.07 us
    ppermute x2, starting transfers between devices, other_core(): return lax.ppermute(x, 'core', [(0, 1), (1, 0)])  5.06 us
    all_to_all x1, waiting for transfers between devices, exchange_16(): return lax.all_to_all(x, axes, 0, 0, tiled=True)  5.03 us
  transfers between devices with their start and end apart: 3, of which 1 were waited for; matrix products, arithmetic and copies ran while one was open for 0% of the time, Pallas kernels for 3%

profile of v3, /device:TPU:1, one launch (start us, length us, event | category | flops | bytes accessed | tf_op | source)
XLA Modules:
  0.0 151.5 jit_solution(2350824230791419347)
XLA Ops:
  0.6 2.0 %shard_map.112 = (bf16[128,1024]{1,0:T(8,128)(2,1)S(1)}, bf16[128,16,128]{2,1,0:T(8,128)(2,1)S(1)}, bf16[128,640]{1,0:T(8,128)(2,1)S(1)}, bf16[4,8,32,128]{3,2,1,0:T(8,128)(2,1)S(1)}, bf16[128,128]{1,0:T(8,128)(2,1)S(1)}) custom-call(bf16[4,8,32,128]{3,2,1,0:T(8,128)(2,1)} %bitcast.26, bf16[128,640]{1,0:T(8,128)(2,1)} %w_ref.1, f32[1,128]{1,0:T(1,128)} %bitcast.31, ...), custom_call_target="tpu_custom_call" | custom-call | flops 134000000 | bytes 2490368 | tf_op jit(solution)/shard_map/pallas_call | solution.py:336
  2.6 0.0 copy-start.4
  2.7 0.0 copy-start.5
  2.7 35.4 %all_to_all.35 = bf16[128,16,128]{2,1,0:T(8,128)(2,1)S(1)} all-to-all(bf16[128,16,128]{2,1,0:T(8,128)(2,1)S(1)} %get-tuple-element.22), channel_id=1, replica_groups=mesh['yl'=2,'x'=4,'core'=2,'z'=8,'yh'=2] {'x','yl','yh','z'}, dimensions={0} | all-to-all | bytes 1048576 | tf_op jit(solution)/shard_map/all_to_all | solution.py:311
  38.1 2.4 %collective-permute-start = (bf16[4,2,2,8,16,128]{5,4,3,2,1,0:T(8,128)(2,1)S(1)}, bf16[4,2,2,8,16,128]{5,4,3,2,1,0:T(8,128)(2,1)S(1)}, u32[]{:S(2)}, u32[]{:S(2)}) collective-permute-start(bf16[4,2,2,8,16,128]{5,4,3,2,1,0:T(8,128)(2,1)S(1)} %bitcast.18), channel_id=1, source_target_pairs={{0,16},{16,0},{1,17},{17,1},{2,18},{18,2},{3,19},{19,3},{4,20},{20... | collective-permute-start | bytes 1572872 | tf_op jit(solution)/shard_map/ppermute | solution.py:315
  41.1 0.0 copy-start.2
  41.1 1.5 %shard_map.113 = (f32[4,128,1024]{2,1,0:T(8,128)S(1)}, f32[128,1024]{1,0:T(8,128)S(1)}, bf16[128,1024]{1,0:T(8,128)(2,1)S(1)}, f32[128,1024]{1,0:T(8,128)S(1)}) custom-call(s32[1,1]{1,0:T(1,128)} %bitcast.16.valid_ref, bf16[128,1024]{1,0:T(8,128)(2,1)S(1)} %get-tuple-element.23.nt_ref, bf16[4,8,32,128]{3,2,1,0:T(8,128)(2,1)S(1)} %get-tuple-element.24.og_ref, ...), custom_call_target="tpu_custom_call" | custom-call | flops 200000000 | bytes 6815744 | tf_op jit(solution)/shard_map/pallas_call | solution.py:357
  42.6 0.0 collective-permute-done.other_ref
  42.6 1.6 %shard_map.114 = (bf16[2,2,4,2,32,512]{5,4,3,2,1,0:T(8,128)(2,1)S(1)}, bf16[4,2,2,4,16,128]{5,4,3,2,1,0:T(8,128)(2,1)S(1)}) custom-call(s32[1,1]{1,0:T(1,128)} %bitcast.17.valid_ref, bf16[4,2,2,8,16,128]{5,4,3,2,1,0:T(8,128)(2,1)S(1)} %bitcast.20, bf16[4,2,2,8,16,128]{5,4,3,2,1,0:T(8,128)(2,1)S(1)} %collective-permute-done.other_ref, ...), custom_call_target="tpu_custom_call" | custom-call | flops 134000000 | bytes 2621440 | tf_op jit(solution)/shard_map/pallas_call | solution.py:363
  44.3 20.4 %all_to_all.36 = bf16[128,8,128]{2,1,0:T(8,128)(2,1)S(1)} all-to-all(bf16[128,8,128]{2,1,0:T(8,128)(2,1)S(1)} %bitcast.29), channel_id=1, replica_groups=mesh['yl'=2,'x'=4,'core'=2,'z'=8,'yh'=2] {'x','yl','yh','z'}, dimensions={0} | all-to-all | bytes 524288 | tf_op jit(solution)/shard_map/all_to_all | solution.py:311
  64.7 0.0 copy-done.4
  64.7 0.0 copy-done.5
  64.7 0.5 shard_map.115
  65.2 18.9 %all_to_all.37 = bf16[128,8,128]{2,1,0:T(8,128)(2,1)S(1)} all-to-all(bf16[128,8,128]{2,1,0:T(8,128)(2,1)S(1)} %bitcast.30), channel_id=1, replica_groups=mesh['yl'=2,'x'=4,'core'=2,'z'=8,'yh'=2] {'x','yl','yh','z'}, dimensions={0} | all-to-all | bytes 524288 | tf_op jit(solution)/shard_map/all_to_all | solution.py:311
  84.0 2.7 %collective-permute-start.1 = (bf16[4,2,2,4,16,128]{5,4,3,2,1,0:T(8,128)(2,1)S(1)}, bf16[4,2,2,4,16,128]{5,4,3,2,1,0:T(8,128)(2,1)S(1)}, u32[]{:S(2)}, u32[]{:S(2)}) collective-permute-start(bf16[4,2,2,4,16,128]{5,4,3,2,1,0:T(8,128)(2,1)S(1)} %bitcast.21), channel_id=1, source_target_pairs={{0,16},{16,0},{1,17},{17,1},{2,18},{18,2},{3,19},{19,3},{4,20},{20... | collective-permute-start | bytes 786440 | tf_op jit(solution)/shard_map/ppermute | solution.py:315
  86.7 0.0 copy-done.2
  86.7 0.5 shard_map.117
  87.2 0.8 shard_map.116
  88.0 0.0 collective-permute-done.1.other_ref
  88.0 0.8 shard_map.118
  88.8 0.0 copy-start
  88.9 0.0 copy-start.1
  88.9 0.0 copy-start.3
  88.9 25.5 %all_to_all.38.grads_ref = bf16[128,16,128]{2,1,0:T(8,128)(2,1)S(1)} all-to-all(bf16[128,16,128]{2,1,0:T(8,128)(2,1)S(1)} %bitcast.24), channel_id=1, replica_groups=mesh['yl'=2,'x'=4,'core'=2,'z'=8,'yh'=2] {'x','yl','yh','z'}, dimensions={0} | all-to-all | bytes 1048576 | tf_op jit(solution)/shard_map/all_to_all | solution.py:311
  114.4 1.4 shard_map.120
  115.8 5.1 %all-to-all-start.4 = ((bf16[16,48,128]{2,1,0:T(8,128)(2,1)}), bf16[16,48,128]{2,1,0:T(8,128)(2,1)S(1)}, u32[]{:S(2)}, u32[]{:S(2)}) async-start(bf16[16,48,128]{2,1,0:T(8,128)(2,1)} %bitcast.14), calls=%async_computation.4 | async-start | bytes 393216 | tf_op jit(solution)/shard_map/all_to_all | solution.py:319
  120.9 0.0 copy-done
  120.9 0.0 copy-done.1
  120.9 0.0 copy-done.3
  120.9 1.7 %shard_map.119._ = bf16[4,8,32,128]{3,2,1,0:T(8,128)(2,1)} custom-call(bf16[128,16,128]{2,1,0:T(8,128)(2,1)S(1)} %all_to_all.38.grads_ref, f32[4,128,1024]{2,1,0:T(8,128)S(1)} %get-tuple-element.37.coef_ref, bf16[128,1024]{1,0:T(8,128)(2,1)S(1)} %get-tuple-element.36._.gg_ref, bf16[4,8,32,128]{3,2,1,0:T(8,128)(2,1)S(1)} %bitcast.27, ...), custom_call_target="tpu_custom_call" | custom-call | flops 168000000 | bytes 524288 | tf_op jit(solution)/shard_map/pallas_call | solution.py:408
  122.6 5.0 %all-to-all-done.4.parts_ref = bf16[16,48,128]{2,1,0:T(8,128)(2,1)S(1)} async-done(((bf16[16,48,128]{2,1,0:T(8,128)(2,1)}), bf16[16,48,128]{2,1,0:T(8,128)(2,1)S(1)}, u32[]{:S(2)}, u32[]{:S(2)}) %all-to-all-start.4) | async-done | bytes 196640 | tf_op jit(solution)/shard_map/all_to_all | solution.py:319
  127.7 11.6 %all_to_all.39.parts_ref = bf16[16,48,128]{2,1,0:T(8,128)(2,1)S(1)} all-to-all(bf16[16,48,128]{2,1,0:T(8,128)(2,1)S(1)} %shard_map.121), channel_id=1, replica_groups=mesh['yl'=2,'x'=4,'core'=2,'z'=8,'yh'=2] {'yh','z'}, dimensions={0} | all-to-all | bytes 393216 | tf_op jit(solution)/shard_map/all_to_all | solution.py:319
  139.3 11.4 %all_to_all.40 = bf16[16,48,128]{2,1,0:T(8,128)(2,1)S(1)} all-to-all(bf16[16,48,128]{2,1,0:T(8,128)(2,1)S(1)} %shard_map.122), channel_id=1, replica_groups=mesh['yl'=2,'x'=4,'core'=2,'z'=8,'yh'=2] {'yl','x','core'}, dimensions={0} | all-to-all | bytes 393216 | tf_op jit(solution)/shard_map/all_to_all | solution.py:319
  150.7 0.8 shard_map.123
  (2 shorter events, 0.1 us)
Async XLA Ops:
  2.6 62.0 %copy-start.4 = (f32[128]{0:T(128)S(1)}, f32[128]{0:T(128)}, u32[]{:S(2)}) copy-start(f32[128]{0:T(128)} %param.16) | copy-start | bytes 1540
  2.7 62.0 %copy-start.5 = (f32[128]{0:T(128)S(1)}, f32[128]{0:T(128)}, u32[]{:S(2)}) copy-start(f32[128]{0:T(128)} %param.17) | copy-start | bytes 1540
  38.1 4.6 %collective-permute-start = (bf16[4,2,2,8,16,128]{5,4,3,2,1,0:T(8,128)(2,1)S(1)}, bf16[4,2,2,8,16,128]{5,4,3,2,1,0:T(8,128)(2,1)S(1)}, u32[]{:S(2)}, u32[]{:S(2)}) collective-permute-start(bf16[4,2,2,8,16,128]{5,4,3,2,1,0:T(8,128)(2,1)S(1)} %bitcast.18), channel_id=1, source_target_pairs={{0,16},{16,0},{1,17},{17,1},{2,18},{18,2},{3,19},{19,3},{4,20},{20... | collective-permute-start | bytes 1572872 | tf_op jit(solution)/shard_map/ppermute | solution.py:315
  41.1 45.6 %copy-start.2 = (bf16[128,128]{1,0:T(8,128)(2,1)S(1)}, bf16[128,128]{1,0:T(8,128)(2,1)}, u32[]{:S(2)}) copy-start(bf16[128,128]{1,0:T(8,128)(2,1)} %wo_ref.1) | copy-start | bytes 98308
  84.0 4.0 %collective-permute-start.1 = (bf16[4,2,2,4,16,128]{5,4,3,2,1,0:T(8,128)(2,1)S(1)}, bf16[4,2,2,4,16,128]{5,4,3,2,1,0:T(8,128)(2,1)S(1)}, u32[]{:S(2)}, u32[]{:S(2)}) collective-permute-start(bf16[4,2,2,4,16,128]{5,4,3,2,1,0:T(8,128)(2,1)S(1)} %bitcast.21), channel_id=1, source_target_pairs={{0,16},{16,0},{1,17},{17,1},{2,18},{18,2},{3,19},{19,3},{4,20},{20... | collective-permute-start | bytes 786440 | tf_op jit(solution)/shard_map/ppermute | solution.py:315
  88.8 32.1 %copy-start = (bf16[32,32,128]{2,1,0:T(8,128)(2,1)S(1)}, bf16[32,32,128]{2,1,0:T(8,128)(2,1)}, u32[]{:S(2)}) copy-start(bf16[32,32,128]{2,1,0:T(8,128)(2,1)} %param.9) | copy-start | bytes 786436
  88.9 32.0 %copy-start.1 = (bf16[128,640]{1,0:T(8,128)(2,1)S(1)}, bf16[128,640]{1,0:T(8,128)(2,1)}, u32[]{:S(2)}) copy-start(bf16[128,640]{1,0:T(8,128)(2,1)} %w_ref.1) | copy-start | bytes 491524
  88.9 32.0 %copy-start.3 = (f32[128]{0:T(128)S(1)}, f32[128]{0:T(128)}, u32[]{:S(2)}) copy-start(f32[128]{0:T(128)} %param.14) | copy-start | bytes 1540
  115.8 11.8 %all-to-all-start.4 = ((bf16[16,48,128]{2,1,0:T(8,128)(2,1)}), bf16[16,48,128]{2,1,0:T(8,128)(2,1)S(1)}, u32[]{:S(2)}, u32[]{:S(2)}) async-start(bf16[16,48,128]{2,1,0:T(8,128)(2,1)} %bitcast.14), calls=%async_computation.4 | async-start | bytes 393216 | tf_op jit(solution)/shard_map/all_to_all | solution.py:319

commit v4 on v3

--- a/solution.py
+++ b/solution.py
@@ -14,6 +14,8 @@
 CHIPS = ("x", "yl", "yh", "z")
 VMEM = pl.BlockSpec(memory_space=pltpu.VMEM)
 HBM = pl.BlockSpec(memory_space=pltpu.HBM)
+ROWS_16 = (2048 + 16, 128)
+ROWS_8 = (1024 + 8, 128)
 ANY = pl.BlockSpec(memory_space=pl.ANY)
 
 
@@ -56,8 +58,8 @@
 
 def load_t(ref, n):
     return jnp.concatenate(
-        [ref[:, q].reshape(128, 128).astype(F32).T for q in (2 * n, 2 * n + 1)], axis=1
-    )
+        [ref[:, q].reshape(128, 128).T for q in (2 * n, 2 * n + 1)], axis=1
+    ).astype(F32)
 
 
 def load_strided(ref, n, first, stride):
@@ -112,17 +114,18 @@
     for copy in copies[4:]:
         copy.start()
     gain, bias = column(gain_ref), column(bias_ref)
+    weights = w_ref[:, :512].T
     for n in range(4):
         x = load_t(x_ref, n)
         unit, _ = norm_unit(x)
         normed = (unit * gain + bias).astype(BF16)
         nt_ref[:, lanes_of(n)] = normed
-        proj = dot(w_ref[:, :512], normed, (0, 0))
+        proj = dot(weights, normed, (1, 0))
         left = jax.nn.sigmoid(proj[128:256]) * proj[:128]
         right = jax.nn.sigmoid(proj[384:512]) * proj[256:384]
         store_strided(scr, n, 0, 16, left)
         store_strided(scr, n, 8, 16, right)
-    lr_ref[...] = scr[...].reshape(128, 16, 128).astype(BF16)
+    lr_ref[...] = scr[:2048].reshape(128, 16, 128).astype(BF16)
     for copy in copies[4:]:
         copy.wait()
 
@@ -130,9 +133,10 @@
 def prepare_kernel(
     valid_ref, nt_ref, og_ref, w_ref, wo_ref, _, coef_ref, back_ref, scaled_ref, gate_ref
 ):
+    weights = w_ref[...].T
     for n in range(4):
         lanes = lanes_of(n)
-        proj = dot(w_ref[...], nt_ref[:, lanes], (0, 0))
+        proj = dot(weights, nt_ref[:, lanes], (1, 0))
         mask = pair_mask(valid_ref[...], n)
         for side in range(2):
             val = proj[256 * side : 256 * side + 128]
@@ -185,13 +189,13 @@
 
 def output_kernel(tri_ref, back_ref, gain_ref, bias_ref, tg_ref, tri16_ref, scr):
     gain, bias = column(gain_ref), column(bias_ref)
-    scr[...] = tri_ref[...].astype(F32).reshape(1024, 128)
+    scr[:1024] = tri_ref[...].astype(F32).reshape(1024, 128)
     for n in range(4):
         unit, rstd = norm_unit(load_strided(scr, n, 0, 8))
         tri16_ref[:, lanes_of(n)] = (unit * gain + bias).astype(BF16)
         grad = norm_backward(back_ref[:, lanes_of(n)], unit, rstd, gain)
         store_strided(scr, n, 0, 8, grad)
-    tg_ref[...] = scr[...].reshape(64, 16, 128).astype(BF16)
+    tg_ref[...] = scr[:1024].reshape(64, 16, 128).astype(BF16)
 
 
 def gate_kernel(tri16_ref, scaled_ref, gate_ref, nt_ref, wo_ref, _, gg_ref, local_ref):
@@ -243,19 +247,26 @@
     return jnp.concatenate(parts, axis=0)
 
 
-def weights_kernel(grads_ref, coef_ref, nt_ref, early_ref, local_ref, scr):
-    scr[...] = grads_ref[...].astype(F32).reshape(2048, 128)
+def weights_kernel(grads_ref, coef_ref, nt_ref, early_ref, mine_ref, theirs_ref, scr, full):
+    scr[:2048] = grads_ref[...].astype(F32).reshape(2048, 128)
     total = None
     for n in range(4):
         local = dot(nt_ref[:, lanes_of(n)], proj_grad(scr, coef_ref, n), (1, 1))
         total = local if total is None else total + local
-    for b in range(4):
-        local_ref[128 * b : 128 * b + 128] = total[:, 128 * b : 128 * b + 128].astype(BF16)
-    local_ref[512:] = early_ref[...].reshape(256, 128).astype(BF16)
-
-
-def input_kernel(grads_ref, coef_ref, gg_ref, x_ref, w_ref, gain_ref, gp_ref, scr):
-    scr[...] = grads_ref[...].astype(F32).reshape(2048, 128)
+    for b in range(6):
+        block = total[:, lanes_t(b)] if b < 4 else early_ref[b - 4]
+        full[b // 3, 128 * (b % 3) : 128 * (b % 3) + 128] = block
+    me = lax.axis_index("core")
+    mine_ref[...] = full[me]
+    theirs_ref[...] = full[1 - me].astype(BF16)
+
+
+def add_cores_kernel(mine_ref, theirs_ref, _, out_ref):
+    out_ref[...] = (mine_ref[...] + theirs_ref[...].astype(F32)).astype(BF16)
+
+
+def input_kernel(grads_ref, coef_ref, gg_ref, x_ref, w_ref, gain_ref, _, gp_ref, scr):
+    scr[:2048] = grads_ref[...].astype(F32).reshape(2048, 128)
     gain = column(gain_ref)
     for n in range(4):
         lanes = lanes_of(n)
@@ -269,27 +280,36 @@
             )
 
 
-def sum_kernel(parts_ref, _, out_ref):
+def sum_kernel(parts_ref, out_ref):
     total = jnp.sum(parts_ref[...].astype(F32), axis=0, keepdims=True).astype(BF16)
     out_ref[...] = jnp.broadcast_to(total, out_ref.shape)
 
 
-def unpack_kernel(total_ref, in_ref, out_ref):
-    for b in range(6):
-        block = total_ref[128 * b : 128 * b + 128].astype(F32) * (1.0 / 512)
-        if b < 5:
-            in_ref[:, 128 * b : 128 * b + 128] = block
-        else:
-            out_ref[...] = block
-
-
-def call(kernel, outs, specs, scratch=(), flops=0):
+def unpack_kernel(total_ref, gp_ref, gp_hbm, in_hbm, out_hbm, in_ref, out_ref, sem):
+    pairs = ((gp_ref, gp_hbm), (in_ref, in_hbm), (out_ref, out_hbm))
+    copies = [pltpu.make_async_copy(src, dst, sem.at[i]) for i, (src, dst) in enumerate(pairs)]
+    copies[0].start()
+    for core in range(2):
+        half = total_ref[:, core].astype(F32).reshape(384, 128) * (1.0 / 512)
+        for i in range(3):
+            b, block = 3 * core + i, half[128 * i : 128 * i + 128]
+            if b < 5:
+                in_ref[:, lanes_t(b)] = block
+            else:
+                out_ref[...] = block
+    for copy in copies[1:]:
+        copy.start()
+    for copy in copies:
+        copy.wait()
+
+
+def call(kernel, outs, specs, scratch=(), flops=0, out_spec=VMEM):
     size = sum(jnp.dtype(d).itemsize * elements(s) for s, d, *_ in outs)
     return pl.pallas_call(
         kernel,
         out_shape=[(where[0] if where else jax.ShapeDtypeStruct)(s, d) for s, d, *where in outs],
         in_specs=specs,
-        out_specs=[VMEM] * len(outs),
+        out_specs=[out_spec] * len(outs),
         scratch_shapes=[pltpu.VMEM(*s) if isinstance(s, tuple) else s for s in scratch],
         compiler_params=pltpu.CompilerParams(vmem_limit_bytes=16 * 1024 * 1024),
         cost_estimate=pl.CostEstimate(flops=flops, bytes_accessed=2 * size, transcendentals=0),
@@ -315,12 +335,12 @@
     return lax.ppermute(x, "core", [(0, 1), (1, 0)])
 
 
-def exchange_16(x, axes):
+def swap(x, axes):
     return lax.all_to_all(x, axes, 0, 0, tiled=True)
 
 
-def add(parts, after):
-    (out,) = call(sum_kernel, [((16, 48, 128), BF16)], [VMEM, HBM])(parts, in_hbm(after))
+def add(parts):
+    (out,) = call(sum_kernel, [((16, 48, 128), BF16)], [VMEM])(parts)
     return out
 
 
@@ -347,7 +367,7 @@
             ((4, 8, 32, 128), BF16),
             ((1, 128), F32),
             ((1, 128), F32),
-            ((2048, 128), F32),
+            (ROWS_16, F32),
             pltpu.SemaphoreType.DMA((6,)),
         ],
         flops=134_000_000,
@@ -371,7 +391,7 @@
         output_kernel,
         [((64, 16, 128), BF16), (tall, BF16)],
         [VMEM] * 4,
-        [((1024, 128), F32)],
+        [(ROWS_8, F32)],
     )(tri.reshape(64, 16, 128), back, out_gain, out_bias)
     own = exchange(tri_grad.reshape(128, 8, 128)).reshape(4, 2, 2, 4, 16, 128)
     other = other_core(own)
@@ -397,26 +417,38 @@
         flops=134_000_000,
     )(other, left_grad, right_grad, mats, gate_grad)
     grads = exchange(grads.reshape(128, 16, 128))
-    (local,) = call(
+    mine, theirs = call(
         weights_kernel,
-        [((768, 128), BF16)],
+        [((384, 128), F32), ((384, 128), BF16)],
         [VMEM] * 4,
-        [((2048, 128), F32)],
+        [(ROWS_16, F32), ((2, 384, 128), F32)],
         flops=134_000_000,
     )(grads, coef, normed_t, early)
-    parts = exchange_16(local.reshape(16, 48, 128), ROW)
+    received = other_core(theirs)
     (grad_pair,) = call(
         input_kernel,
-        [((4, 8, 32, 128), BF16, pltpu.HBM)],
-        [VMEM] * 6,
-        [((2048, 128), F32)],
+        [((4, 8, 32, 128), BF16, pltpu.VMEM)],
+        [VMEM] * 6 + [ANY],
+        [(ROWS_16, F32)],
         flops=168_000_000,
-    )(grads, coef, gate_grad, x, w_in, in_gain)
-    parts = exchange_16(add(parts, grad_pair), ("yh", "z"))
-    parts = exchange_16(add(parts, grad_pair), ROW)
-    grad_in, grad_out = call(
-        unpack_kernel, [((128, 640), F32), ((128, 128), F32)], [VMEM]
-    )(parts.reshape(768, 128))
+    )(grads, coef, gate_grad, x, w_in, in_gain, theirs)
+    (chip,) = call(add_cores_kernel, [((384, 128), BF16)], [VMEM, VMEM, ANY])(
+        mine, received, grad_pair
+    )
+    parts = swap(chip.reshape(8, 48, 128), ("yl", "x"))
+    parts = swap(add(parts), ("yh", "z"))
+    parts = swap(add(parts), ROW)
+    grad_pair, grad_in, grad_out = call(
+        unpack_kernel,
+        [
+            ((4, 8, 32, 128), BF16, pltpu.HBM),
+            ((128, 640), F32, pltpu.HBM),
+            ((128, 128), F32, pltpu.HBM),
+        ],
+        [VMEM] * 2,
+        [((128, 640), F32), ((128, 128), F32), pltpu.SemaphoreType.DMA((3,))],
+        out_spec=HBM,
+    )(parts.reshape(8, 2, 48, 128), grad_pair)
     return grad_pair.reshape(32, 32, 128), grad_in, grad_out
 
 

time: 152 us -> 151 us (level)
  blocking collectives: 123 us -> 132 us
  waiting for transfers between devices: 5.03 us -> 0.01 us
  starting transfers between devices: 10.1 us -> 6.92 us
    all_to_all x2 -> x3, blocking collectives: 23 us -> 31.8 us  [swap(): return lax.all_to_all(x, axes, 0, 0, tiled=True)]
    all_to_all x1 -> x0, starting transfers between devices: 5.07 us -> none  [exchange_16(): return lax.all_to_all(x, axes, 0, 0, tiled=True)]
    all_to_all x1 -> x0, waiting for transfers between devices: 5.03 us -> none  [exchange_16(): return lax.all_to_all(x, axes, 0, 0, tiled=True)]
    ppermute x2 -> x3, starting transfers between devices: 5.06 us -> 6.92 us  [other_core(): return lax.ppermute(x, 'core', [(0, 1), (1, 0)])]
    pallas_call x5 -> x6, Pallas kernels: 3.92 us -> 2.72 us  [the longest x1 0.99 us: shards(): call(input_kernel, [((4, 8, 32, 128), BF16, pltpu.VMEM)], [VMEM] * 6 + [A...]
  transfers between devices with their start and end apart: 3 -> 3, of which waited for: 1 -> 0; matrix products, arithmetic and copies ran while one was open for 0% -> 0% of each run, Pallas kernels for 3% -> 2%
where the time goes in v4:
time: 151 us
  blocking collectives  132 us (87%)
  Pallas kernels  10.4 us (7%)
  starting transfers between devices  6.92 us (5%)
  between operations  1.59 us (1%)
    all_to_all x4, blocking collectives, exchange(): return lax.all_to_all(x, CHIPS, 0, 0, tiled=True)  100 us
    all_to_all x3, blocking collectives, swap(): return lax.all_to_all(x, axes, 0, 0, tiled=True)  31.8 us
    ppermute x3, starting transfers between devices, other_core(): return lax.ppermute(x, 'core', [(0, 1), (1, 0)])  6.92 us
  transfers between devices with their start and end apart: 3, of which 0 were waited for; matrix products, arithmetic and copies ran while one was open for 0% of the time, Pallas kernels for 2%

profile of v4, /device:TPU:1, one launch (start us, length us, event | category | flops | bytes accessed | tf_op | source)
XLA Modules:
  0.0 150.9 jit_solution(10562207521832011868)
XLA Ops:
  0.6 2.0 %shard_map.112 = (bf16[128,1024]{1,0:T(8,128)(2,1)S(1)}, bf16[128,16,128]{2,1,0:T(8,128)(2,1)S(1)}, bf16[128,640]{1,0:T(8,128)(2,1)S(1)}, bf16[4,8,32,128]{3,2,1,0:T(8,128)(2,1)S(1)}, bf16[128,128]{1,0:T(8,128)(2,1)S(1)}) custom-call(bf16[4,8,32,128]{3,2,1,0:T(8,128)(2,1)} %bitcast.26, bf16[128,640]{1,0:T(8,128)(2,1)} %w_ref.1, f32[1,128]{1,0:T(1,128)} %bitcast.32, ...), custom_call_target="tpu_custom_call" | custom-call | flops 134000000 | bytes 2490368 | tf_op jit(solution)/shard_map/pallas_call | solution.py:356
  2.6 0.0 copy-start.4
  2.7 0.0 copy-start.5
  2.7 35.4 %all_to_all.35 = bf16[128,16,128]{2,1,0:T(8,128)(2,1)S(1)} all-to-all(bf16[128,16,128]{2,1,0:T(8,128)(2,1)S(1)} %get-tuple-element.25), channel_id=1, replica_groups=mesh['yl'=2,'x'=4,'core'=2,'z'=8,'yh'=2] {'x','yl','yh','z'}, dimensions={0} | all-to-all | bytes 1048576 | tf_op jit(solution)/shard_map/all_to_all | solution.py:331
  38.1 2.4 %collective-permute-start = (bf16[4,2,2,8,16,128]{5,4,3,2,1,0:T(8,128)(2,1)S(1)}, bf16[4,2,2,8,16,128]{5,4,3,2,1,0:T(8,128)(2,1)S(1)}, u32[]{:S(2)}, u32[]{:S(2)}) collective-permute-start(bf16[4,2,2,8,16,128]{5,4,3,2,1,0:T(8,128)(2,1)S(1)} %bitcast.18), channel_id=1, source_target_pairs={{0,16},{16,0},{1,17},{17,1},{2,18},{18,2},{3,19},{19,3},{4,20},{20... | collective-permute-start | bytes 1572872 | tf_op jit(solution)/shard_map/ppermute | solution.py:335
  41.1 0.0 copy-start.2
  41.1 1.5 shard_map.113
  42.6 0.0 collective-permute-done.other_ref
  42.6 1.6 %shard_map.114 = (bf16[2,2,4,2,32,512]{5,4,3,2,1,0:T(8,128)(2,1)S(1)}, bf16[4,2,2,4,16,128]{5,4,3,2,1,0:T(8,128)(2,1)S(1)}) custom-call(s32[1,1]{1,0:T(1,128)} %bitcast.17.valid_ref, bf16[4,2,2,8,16,128]{5,4,3,2,1,0:T(8,128)(2,1)S(1)} %bitcast.20, bf16[4,2,2,8,16,128]{5,4,3,2,1,0:T(8,128)(2,1)S(1)} %collective-permute-done.other_ref, ...), custom_call_target="tpu_custom_call" | custom-call | flops 134000000 | bytes 2621440 | tf_op jit(solution)/shard_map/pallas_call | solution.py:383
  44.2 20.4 %all_to_all.36 = bf16[128,8,128]{2,1,0:T(8,128)(2,1)S(1)} all-to-all(bf16[128,8,128]{2,1,0:T(8,128)(2,1)S(1)} %bitcast.30), channel_id=1, replica_groups=mesh['yl'=2,'x'=4,'core'=2,'z'=8,'yh'=2] {'x','yl','yh','z'}, dimensions={0} | all-to-all | bytes 524288 | tf_op jit(solution)/shard_map/all_to_all | solution.py:331
  64.6 0.0 copy-done.4
  64.6 0.0 copy-done.5
  64.6 0.5 shard_map.115
  65.1 18.9 %all_to_all.37 = bf16[128,8,128]{2,1,0:T(8,128)(2,1)S(1)} all-to-all(bf16[128,8,128]{2,1,0:T(8,128)(2,1)S(1)} %bitcast.31), channel_id=1, replica_groups=mesh['yl'=2,'x'=4,'core'=2,'z'=8,'yh'=2] {'x','yl','yh','z'}, dimensions={0} | all-to-all | bytes 524288 | tf_op jit(solution)/shard_map/all_to_all | solution.py:331
  84.0 2.7 %collective-permute-start.1 = (bf16[4,2,2,4,16,128]{5,4,3,2,1,0:T(8,128)(2,1)S(1)}, bf16[4,2,2,4,16,128]{5,4,3,2,1,0:T(8,128)(2,1)S(1)}, u32[]{:S(2)}, u32[]{:S(2)}) collective-permute-start(bf16[4,2,2,4,16,128]{5,4,3,2,1,0:T(8,128)(2,1)S(1)} %bitcast.21), channel_id=1, source_target_pairs={{0,16},{16,0},{1,17},{17,1},{2,18},{18,2},{3,19},{19,3},{4,20},{20... | collective-permute-start | bytes 786440 | tf_op jit(solution)/shard_map/ppermute | solution.py:335
  86.7 0.0 copy-done.2
  86.7 0.5 shard_map.117
  87.1 0.8 shard_map.116
  87.9 0.0 collective-permute-done.1.other_ref
  88.0 0.8 shard_map.118
  88.8 0.0 copy-start
  88.8 0.0 copy-start.1
  88.8 0.0 copy-start.3
  88.8 25.5 %all_to_all.38.grads_ref = bf16[128,16,128]{2,1,0:T(8,128)(2,1)S(1)} all-to-all(bf16[128,16,128]{2,1,0:T(8,128)(2,1)S(1)} %bitcast.24), channel_id=1, replica_groups=mesh['yl'=2,'x'=4,'core'=2,'z'=8,'yh'=2] {'x','yl','yh','z'}, dimensions={0} | all-to-all | bytes 1048576 | tf_op jit(solution)/shard_map/all_to_all | solution.py:331
  114.4 0.8 shard_map.119
  115.2 1.9 %collective-permute-start.2 = (bf16[384,128]{1,0:T(8,128)(2,1)S(1)}, bf16[384,128]{1,0:T(8,128)(2,1)S(1)}, u32[]{:S(2)}, u32[]{:S(2)}) collective-permute-start(bf16[384,128]{1,0:T(8,128)(2,1)S(1)} %get-tuple-element.43._), channel_id=1, source_target_pairs={{0,16},{16,0},{1,17},{17,1},{2,18},{18,2},{3,19},{19,3},{4,20},{20... | collective-permute-start | bytes 294920 | tf_op jit(solution)/shard_map/ppermute | solution.py:335
  117.0 0.0 copy-done
  117.0 0.0 copy-done.1
  117.0 0.0 copy-done.3
  117.0 1.0 shard_map.120._.gp_ref
  118.0 0.0 collective-permute-done.2.theirs_ref
  118.1 7.7 %all_to_all.39.parts_ref = bf16[8,48,128]{2,1,0:T(8,128)(2,1)S(1)} all-to-all(bf16[8,48,128]{2,1,0:T(8,128)(2,1)S(1)} %bitcast.29), channel_id=1, replica_groups=mesh['yl'=2,'x'=4,'core'=2,'z'=8,'yh'=2] {'yl','x'}, dimensions={0} | all-to-all | bytes 196608 | tf_op jit(solution)/shard_map/all_to_all | solution.py:339
  125.8 11.8 %all_to_all.40.parts_ref = bf16[16,48,128]{2,1,0:T(8,128)(2,1)S(1)} all-to-all(bf16[16,48,128]{2,1,0:T(8,128)(2,1)S(1)} %shard_map.122), channel_id=1, replica_groups=mesh['yl'=2,'x'=4,'core'=2,'z'=8,'yh'=2] {'yh','z'}, dimensions={0} | all-to-all | bytes 393216 | tf_op jit(solution)/shard_map/all_to_all | solution.py:339
  137.6 12.3 %all_to_all.41 = bf16[16,48,128]{2,1,0:T(8,128)(2,1)S(1)} all-to-all(bf16[16,48,128]{2,1,0:T(8,128)(2,1)S(1)} %shard_map.123), channel_id=1, replica_groups=mesh['yl'=2,'x'=4,'core'=2,'z'=8,'yh'=2] {'yl','x','core'}, dimensions={0} | all-to-all | bytes 393216 | tf_op jit(solution)/shard_map/all_to_all | solution.py:339
  149.9 0.8 shard_map.124
  (3 shorter events, 0.1 us)
Async XLA Ops:
  2.6 62.0 %copy-start.4 = (f32[128]{0:T(128)S(1)}, f32[128]{0:T(128)}, u32[]{:S(2)}) copy-start(f32[128]{0:T(128)} %param.16) | copy-start | bytes 1540
  2.7 62.0 %copy-start.5 = (f32[128]{0:T(128)S(1)}, f32[128]{0:T(128)}, u32[]{:S(2)}) copy-start(f32[128]{0:T(128)} %param.17) | copy-start | bytes 1540
  38.1 4.5 %collective-permute-start = (bf16[4,2,2,8,16,128]{5,4,3,2,1,0:T(8,128)(2,1)S(1)}, bf16[4,2,2,8,16,128]{5,4,3,2,1,0:T(8,128)(2,1)S(1)}, u32[]{:S(2)}, u32[]{:S(2)}) collective-permute-start(bf16[4,2,2,8,16,128]{5,4,3,2,1,0:T(8,128)(2,1)S(1)} %bitcast.18), channel_id=1, source_target_pairs={{0,16},{16,0},{1,17},{17,1},{2,18},{18,2},{3,19},{19,3},{4,20},{20... | collective-permute-start | bytes 1572872 | tf_op jit(solution)/shard_map/ppermute | solution.py:335
  41.1 45.6 %copy-start.2 = (bf16[128,128]{1,0:T(8,128)(2,1)S(1)}, bf16[128,128]{1,0:T(8,128)(2,1)}, u32[]{:S(2)}) copy-start(bf16[128,128]{1,0:T(8,128)(2,1)} %wo_ref.1) | copy-start | bytes 98308
  84.0 4.0 %collective-permute-start.1 = (bf16[4,2,2,4,16,128]{5,4,3,2,1,0:T(8,128)(2,1)S(1)}, bf16[4,2,2,4,16,128]{5,4,3,2,1,0:T(8,128)(2,1)S(1)}, u32[]{:S(2)}, u32[]{:S(2)}) collective-permute-start(bf16[4,2,2,4,16,128]{5,4,3,2,1,0:T(8,128)(2,1)S(1)} %bitcast.21), channel_id=1, source_target_pairs={{0,16},{16,0},{1,17},{17,1},{2,18},{18,2},{3,19},{19,3},{4,20},{20... | collective-permute-start | bytes 786440 | tf_op jit(solution)/shard_map/ppermute | solution.py:335
  88.8 28.2 %copy-start = (bf16[32,32,128]{2,1,0:T(8,128)(2,1)S(1)}, bf16[32,32,128]{2,1,0:T(8,128)(2,1)}, u32[]{:S(2)}) copy-start(bf16[32,32,128]{2,1,0:T(8,128)(2,1)} %param.9) | copy-start | bytes 786436
  88.8 28.2 %copy-start.1 = (bf16[128,640]{1,0:T(8,128)(2,1)S(1)}, bf16[128,640]{1,0:T(8,128)(2,1)}, u32[]{:S(2)}) copy-start(bf16[128,640]{1,0:T(8,128)(2,1)} %w_ref.1) | copy-start | bytes 491524
  88.8 28.2 %copy-start.3 = (f32[128]{0:T(128)S(1)}, f32[128]{0:T(128)}, u32[]{:S(2)}) copy-start(f32[128]{0:T(128)} %param.14) | copy-start | bytes 1540
  115.2 2.9 %collective-permute-start.2 = (bf16[384,128]{1,0:T(8,128)(2,1)S(1)}, bf16[384,128]{1,0:T(8,128)(2,1)S(1)}, u32[]{:S(2)}, u32[]{:S(2)}) collective-permute-start(bf16[384,128]{1,0:T(8,128)(2,1)S(1)} %get-tuple-element.43._), channel_id=1, source_target_pairs={{0,16},{16,0},{1,17},{17,1},{2,18},{18,2},{3,19},{19,3},{4,20},{20... | collective-permute-start | bytes 294920 | tf_op jit(solution)/shard_map/ppermute | solution.py:335

commit v5 on v4

--- a/solution.py
+++ b/solution.py
@@ -163,23 +163,40 @@
     return to_blocks(matrix[:, :16, lanes_t(t)], matrix[:, 16:, lanes_t(t)])
 
 
-def triangle_kernel(valid_ref, own_ref, other_ref, _, mats_ref, tri_ref):
+def assemble(ref, core, valid, outs):
+    dims = (8, 16, 128)
+    block, row, lane = (lax.broadcasted_iota(jnp.int32, dims, d) for d in range(3))
+    token = 64 * block + row + 32 * core
+    valid = jnp.broadcast_to(valid, dims)
+    for t in range(4):
+        sides = [swap_rows(by_yl(ref, yh, 2 * t), by_yl(ref, yh, 2 * t + 1)) for yh in range(2)]
+        for side, out in outs:
+            for h, values in enumerate(to_rows(sides[0][side], sides[1][side])):
+                keep = (token + 16 * h < valid) & (lane + 128 * t < valid)
+                values = jnp.where(keep, values, jnp.zeros_like(values))
+                out(slice(16 * h, 16 * h + 16), lanes_t(t), values.reshape(2, 4, 16, 128))
+
+
+def store_in(ref, core=None):
+    def store(rows, lanes, values):
+        if core is None:
+            ref[:, :, rows, lanes] = values
+        else:
+            ref[:, :, core, rows, lanes] = values
+
+    return store
+
+
+def triangle_kernel(
+    valid_ref, own_ref, other_ref, _, left_ref, right_ref, tri_ref, valid_near_ref
+):
     me = lax.axis_index("core")
-    dims = (8, 16, 128)
-    valid = jnp.broadcast_to(valid_ref[...].reshape(1, 1, 1), dims)
-    block, row, lane = (lax.broadcasted_iota(jnp.int32, dims, d) for d in range(3))
-    for ref, core in ((own_ref, me), (other_ref, 1 - me)):
-        token = 64 * block + row + 32 * core
-        for t in range(4):
-            sides = [swap_rows(by_yl(ref, yh, 2 * t), by_yl(ref, yh, 2 * t + 1)) for yh in range(2)]
-            for side in range(2):
-                for h, values in enumerate(to_rows(sides[0][side], sides[1][side])):
-                    keep = (token + 16 * h < valid) & (lane + 128 * t < valid)
-                    mats_ref[side, :, :, core, 16 * h : 16 * h + 16, lanes_t(t)] = jnp.where(
-                        keep, values, jnp.zeros_like(values)
-                    ).reshape(2, 4, 16, 128)
-    left = mats_ref[0, :, :, me].reshape(256, 512)
-    right = mats_ref[1].reshape(512, 512)
+    valid = valid_ref[...].reshape(1, 1, 1)
+    valid_near_ref[...] = jnp.broadcast_to(valid_ref[...], (8, 128))
+    assemble(own_ref, me, valid, ((0, store_in(left_ref)), (1, store_in(right_ref, me))))
+    assemble(other_ref, 1 - me, valid, ((1, store_in(right_ref, 1 - me)),))
+    left = left_ref[...].reshape(256, 512)
+    right = right_ref[...].reshape(512, 512)
     tri = dot(left, right, (1, 1)).astype(BF16).reshape(8, 32, 512)
     for t in range(4):
         for yh, block in enumerate(matrix_blocks(tri, t)):
@@ -212,25 +229,32 @@
             out[:, :, 16 * h : 16 * h + 16, lanes_t(t)] = values.reshape(2, 4, 16, 128)
 
 
-def own_grads_kernel(own_ref, mats_ref, lg_ref, rg_ref, tg, full):
+def own_columns(tg, turned, me):
+    turned[...] = tg[...].reshape(256, 512).T.reshape(2, 4, 2, 32, 256)
+    return turned[:, :, me].reshape(256, 256)
+
+
+def own_grads_kernel(
+    own_ref, left_ref, right_ref, blocks_ref, valid_ref, lg_ref, rg_ref, rest_ref, tg, turned
+):
     me = lax.axis_index("core")
     assemble_grad(own_ref, tg)
     grad = tg[...].reshape(256, 512)
-    left_grad = dot(grad, mats_ref[1].reshape(512, 512), (1, 0)).astype(BF16).reshape(8, 32, 512)
+    right = right_ref[...].reshape(512, 512)
+    left_grad = dot(grad, right, (1, 0)).astype(BF16).reshape(8, 32, 512)
     for t in range(4):
         for yh, block in enumerate(matrix_blocks(left_grad, t)):
             lg_ref[t, yh] = block
-    left = mats_ref[0, :, :, me].reshape(256, 512)
-    full[...] = dot(grad, left, (0, 0)).reshape(2, 4, 2, 32, 512)
-    rg_ref[...] = full[:, :, me]
-
-
-def grads_kernel(other_ref, lg_ref, rg_ref, mats_ref, _, out_ref, tg, full):
+    rg_ref[...] = dot(own_columns(tg, turned, me), left_ref[...].reshape(256, 512), (1, 0))
+    valid = valid_ref[:1, :].reshape(1, 1, 128)
+    assemble(blocks_ref, 1 - me, valid, ((0, store_in(rest_ref)),))
+
+
+def grads_kernel(other_ref, lg_ref, rg_ref, rest_ref, _, out_ref, tg, turned):
     me = lax.axis_index("core")
     assemble_grad(other_ref, tg)
-    left = mats_ref[0, :, :, 1 - me].reshape(256, 512)
-    full[...] = dot(tg[...].reshape(256, 512), left, (0, 0)).reshape(2, 4, 2, 32, 512)
-    right_grad = (full[:, :, me] + rg_ref[...]).astype(BF16).reshape(8, 32, 512)
+    right_grad = dot(own_columns(tg, turned, me), rest_ref[...].reshape(256, 512), (1, 0))
+    right_grad = (right_grad + rg_ref[...]).astype(BF16).reshape(8, 32, 512)
     for t in range(4):
         for yh, block in enumerate(matrix_blocks(right_grad, t)):
             for z, both in enumerate(swap_rows(lg_ref[t, yh], block)):
@@ -380,9 +404,15 @@
         [VMEM] * 5 + [ANY],
         flops=200_000_000,
     )(valid, normed_t, y_near, w_near, w_out_near, own)
-    mats, tri = call(
+    blocks = other
+    left, right, tri, valid = call(
         triangle_kernel,
-        [((2, 2, 4, 2, 32, 512), BF16), ((4, 2, 2, 4, 16, 128), BF16)],
+        [
+            (matrix, BF16),
+            ((2, 4, 2, 32, 512), BF16),
+            ((4, 2, 2, 4, 16, 128), BF16),
+            ((8, 128), jnp.int32),
+        ],
         [VMEM] * 3 + [ANY],
         flops=134_000_000,
     )(valid, own, other, back)
@@ -401,21 +431,21 @@
         [VMEM] * 5 + [ANY],
         flops=100_000_000,
     )(tri16, scaled, gate, normed_t, w_out, own)
-    scratch = [(matrix, BF16), ((2, 4, 2, 32, 512), F32)]
-    left_grad, right_grad = call(
+    scratch = [(matrix, BF16), ((2, 4, 2, 32, 256), BF16)]
+    left_grad, right_grad, rest = call(
         own_grads_kernel,
-        [((4, 2, 8, 16, 128), BF16), (matrix, F32)],
-        [VMEM] * 2,
+        [((4, 2, 8, 16, 128), BF16), ((256, 512), F32), (matrix, BF16)],
+        [VMEM] * 5,
         scratch,
-        flops=268_000_000,
-    )(own, mats)
+        flops=200_000_000,
+    )(own, left, right, blocks, valid)
     (grads,) = call(
         grads_kernel,
         [((4, 2, 2, 8, 16, 128), BF16)],
         [VMEM] * 4 + [ANY],
         scratch,
         flops=134_000_000,
-    )(other, left_grad, right_grad, mats, gate_grad)
+    )(other, left_grad, right_grad, rest, gate_grad)
     grads = exchange(grads.reshape(128, 16, 128))
     mine, theirs = call(
         weights_kernel,

time: 151 us -> 151 us (level)
  transfers between devices with their start and end apart: 3 -> 3, of which waited for: 0 -> 0; matrix products, arithmetic and copies ran while one was open for 0% -> 0% of each run, Pallas kernels for 2% -> 3%
where the time goes in v5:
time: 151 us
  blocking collectives  132 us (87%)
  Pallas kernels  9.95 us (7%)
  starting transfers between devices  6.72 us (4%)
  between operations  1.59 us (1%)
    all_to_all x4, blocking collectives, exchange(): return lax.all_to_all(x, CHIPS, 0, 0, tiled=True)  101 us
    all_to_all x3, blocking collectives, swap(): return lax.all_to_all(x, axes, 0, 0, tiled=True)  31.7 us
    ppermute x3, starting transfers between devices, other_core(): return lax.ppermute(x, 'core', [(0, 1), (1, 0)])  6.72 us
  transfers between devices with their start and end apart: 3, of which 0 were waited for; matrix products, arithmetic and copies ran while one was open for 0% of the time, Pallas kernels for 3%

profile of v5, /device:TPU:1, one launch (start us, length us, event | category | flops | bytes accessed | tf_op | source)
XLA Modules:
  0.0 150.6 jit_solution(11024144462805082865)
XLA Ops:
  0.6 2.0 %shard_map.112 = (bf16[128,1024]{1,0:T(8,128)(2,1)S(1)}, bf16[128,16,128]{2,1,0:T(8,128)(2,1)S(1)}, bf16[128,640]{1,0:T(8,128)(2,1)S(1)}, bf16[4,8,32,128]{3,2,1,0:T(8,128)(2,1)S(1)}, bf16[128,128]{1,0:T(8,128)(2,1)S(1)}) custom-call(bf16[4,8,32,128]{3,2,1,0:T(8,128)(2,1)} %bitcast.26, bf16[128,640]{1,0:T(8,128)(2,1)} %w_ref.1, f32[1,128]{1,0:T(1,128)} %bitcast.32, ...), custom_call_target="tpu_custom_call" | custom-call | flops 134000000 | bytes 2490368 | tf_op jit(solution)/shard_map/pallas_call | solution.py:380
  2.6 0.0 copy-start.4
  2.7 0.0 copy-start.5
  2.7 35.4 %all_to_all.35 = bf16[128,16,128]{2,1,0:T(8,128)(2,1)S(1)} all-to-all(bf16[128,16,128]{2,1,0:T(8,128)(2,1)S(1)} %get-tuple-element.28), channel_id=1, replica_groups=mesh['yl'=2,'x'=4,'core'=2,'z'=8,'yh'=2] {'x','yl','yh','z'}, dimensions={0} | all-to-all | bytes 1048576 | tf_op jit(solution)/shard_map/all_to_all | solution.py:355
  38.1 2.4 %collective-permute-start = (bf16[4,2,2,8,16,128]{5,4,3,2,1,0:T(8,128)(2,1)S(1)}, bf16[4,2,2,8,16,128]{5,4,3,2,1,0:T(8,128)(2,1)S(1)}, u32[]{:S(2)}, u32[]{:S(2)}) collective-permute-start(bf16[4,2,2,8,16,128]{5,4,3,2,1,0:T(8,128)(2,1)S(1)} %bitcast.18), channel_id=1, source_target_pairs={{0,16},{16,0},{1,17},{17,1},{2,18},{18,2},{3,19},{19,3},{4,20},{20... | collective-permute-start | bytes 1572872 | tf_op jit(solution)/shard_map/ppermute | solution.py:359
  41.1 0.0 copy-start.2
  41.1 1.5 shard_map.113
  42.6 0.0 collective-permute-done.other_ref.blocks_ref
  42.6 1.2 shard_map.114
  43.8 20.4 %all_to_all.36 = bf16[128,8,128]{2,1,0:T(8,128)(2,1)S(1)} all-to-all(bf16[128,8,128]{2,1,0:T(8,128)(2,1)S(1)} %bitcast.30), channel_id=1, replica_groups=mesh['yl'=2,'x'=4,'core'=2,'z'=8,'yh'=2] {'x','yl','yh','z'}, dimensions={0} | all-to-all | bytes 524288 | tf_op jit(solution)/shard_map/all_to_all | solution.py:355
  64.2 0.0 copy-done.4
  64.2 0.0 copy-done.5
  64.2 0.5 shard_map.115
  64.7 18.9 %all_to_all.37 = bf16[128,8,128]{2,1,0:T(8,128)(2,1)S(1)} all-to-all(bf16[128,8,128]{2,1,0:T(8,128)(2,1)S(1)} %bitcast.31), channel_id=1, replica_groups=mesh['yl'=2,'x'=4,'core'=2,'z'=8,'yh'=2] {'x','yl','yh','z'}, dimensions={0} | all-to-all | bytes 524288 | tf_op jit(solution)/shard_map/all_to_all | solution.py:355
  83.5 2.7 %collective-permute-start.1 = (bf16[4,2,2,4,16,128]{5,4,3,2,1,0:T(8,128)(2,1)S(1)}, bf16[4,2,2,4,16,128]{5,4,3,2,1,0:T(8,128)(2,1)S(1)}, u32[]{:S(2)}, u32[]{:S(2)}) collective-permute-start(bf16[4,2,2,4,16,128]{5,4,3,2,1,0:T(8,128)(2,1)S(1)} %bitcast.21), channel_id=1, source_target_pairs={{0,16},{16,0},{1,17},{17,1},{2,18},{18,2},{3,19},{19,3},{4,20},{20... | collective-permute-start | bytes 786440 | tf_op jit(solution)/shard_map/ppermute | solution.py:359
  86.2 0.0 copy-done.2
  86.2 0.5 shard_map.117
  86.7 1.0 shard_map.116
  87.6 0.0 collective-permute-done.1.other_ref
  87.7 0.6 shard_map.118
  88.3 0.0 copy-start
  88.3 0.0 copy-start.1
  88.3 0.0 copy-start.3
  88.3 25.9 %all_to_all.38.grads_ref = bf16[128,16,128]{2,1,0:T(8,128)(2,1)S(1)} all-to-all(bf16[128,16,128]{2,1,0:T(8,128)(2,1)S(1)} %bitcast.24), channel_id=1, replica_groups=mesh['yl'=2,'x'=4,'core'=2,'z'=8,'yh'=2] {'x','yl','yh','z'}, dimensions={0} | all-to-all | bytes 1048576 | tf_op jit(solution)/shard_map/all_to_all | solution.py:355
  114.3 0.8 shard_map.119
  115.1 1.7 %collective-permute-start.2 = (bf16[384,128]{1,0:T(8,128)(2,1)S(1)}, bf16[384,128]{1,0:T(8,128)(2,1)S(1)}, u32[]{:S(2)}, u32[]{:S(2)}) collective-permute-start(bf16[384,128]{1,0:T(8,128)(2,1)S(1)} %get-tuple-element.49._), channel_id=1, source_target_pairs={{0,16},{16,0},{1,17},{17,1},{2,18},{18,2},{3,19},{19,3},{4,20},{20... | collective-permute-start | bytes 294920 | tf_op jit(solution)/shard_map/ppermute | solution.py:359
  116.7 0.0 copy-done
  116.7 0.0 copy-done.1
  116.7 0.0 copy-done.3
  116.7 1.0 shard_map.120._.gp_ref
  117.7 0.0 collective-permute-done.2.theirs_ref
  117.8 7.7 %all_to_all.39.parts_ref = bf16[8,48,128]{2,1,0:T(8,128)(2,1)S(1)} all-to-all(bf16[8,48,128]{2,1,0:T(8,128)(2,1)S(1)} %bitcast.29), channel_id=1, replica_groups=mesh['yl'=2,'x'=4,'core'=2,'z'=8,'yh'=2] {'yl','x'}, dimensions={0} | all-to-all | bytes 196608 | tf_op jit(solution)/shard_map/all_to_all | solution.py:363
  125.5 11.7 %all_to_all.40.parts_ref = bf16[16,48,128]{2,1,0:T(8,128)(2,1)S(1)} all-to-all(bf16[16,48,128]{2,1,0:T(8,128)(2,1)S(1)} %shard_map.122), channel_id=1, replica_groups=mesh['yl'=2,'x'=4,'core'=2,'z'=8,'yh'=2] {'yh','z'}, dimensions={0} | all-to-all | bytes 393216 | tf_op jit(solution)/shard_map/all_to_all | solution.py:363
  137.2 12.3 %all_to_all.41 = bf16[16,48,128]{2,1,0:T(8,128)(2,1)S(1)} all-to-all(bf16[16,48,128]{2,1,0:T(8,128)(2,1)S(1)} %shard_map.123), channel_id=1, replica_groups=mesh['yl'=2,'x'=4,'core'=2,'z'=8,'yh'=2] {'yl','x','core'}, dimensions={0} | all-to-all | bytes 393216 | tf_op jit(solution)/shard_map/all_to_all | solution.py:363
  149.6 0.8 shard_map.124
  (3 shorter events, 0.1 us)
Async XLA Ops:
  2.6 61.5 %copy-start.4 = (f32[128]{0:T(128)S(1)}, f32[128]{0:T(128)}, u32[]{:S(2)}) copy-start(f32[128]{0:T(128)} %param.16) | copy-start | bytes 1540
  2.7 61.5 %copy-start.5 = (f32[128]{0:T(128)S(1)}, f32[128]{0:T(128)}, u32[]{:S(2)}) copy-start(f32[128]{0:T(128)} %param.17) | copy-start | bytes 1540
  38.1 4.5 %collective-permute-start = (bf16[4,2,2,8,16,128]{5,4,3,2,1,0:T(8,128)(2,1)S(1)}, bf16[4,2,2,8,16,128]{5,4,3,2,1,0:T(8,128)(2,1)S(1)}, u32[]{:S(2)}, u32[]{:S(2)}) collective-permute-start(bf16[4,2,2,8,16,128]{5,4,3,2,1,0:T(8,128)(2,1)S(1)} %bitcast.18), channel_id=1, source_target_pairs={{0,16},{16,0},{1,17},{17,1},{2,18},{18,2},{3,19},{19,3},{4,20},{20... | collective-permute-start | bytes 1572872 | tf_op jit(solution)/shard_map/ppermute | solution.py:359
  41.1 45.1 %copy-start.2 = (bf16[128,128]{1,0:T(8,128)(2,1)S(1)}, bf16[128,128]{1,0:T(8,128)(2,1)}, u32[]{:S(2)}) copy-start(bf16[128,128]{1,0:T(8,128)(2,1)} %wo_ref.1) | copy-start | bytes 98308
  83.5 4.1 %collective-permute-start.1 = (bf16[4,2,2,4,16,128]{5,4,3,2,1,0:T(8,128)(2,1)S(1)}, bf16[4,2,2,4,16,128]{5,4,3,2,1,0:T(8,128)(2,1)S(1)}, u32[]{:S(2)}, u32[]{:S(2)}) collective-permute-start(bf16[4,2,2,4,16,128]{5,4,3,2,1,0:T(8,128)(2,1)S(1)} %bitcast.21), channel_id=1, source_target_pairs={{0,16},{16,0},{1,17},{17,1},{2,18},{18,2},{3,19},{19,3},{4,20},{20... | collective-permute-start | bytes 786440 | tf_op jit(solution)/shard_map/ppermute | solution.py:359
  88.3 28.4 %copy-start = (bf16[32,32,128]{2,1,0:T(8,128)(2,1)S(1)}, bf16[32,32,128]{2,1,0:T(8,128)(2,1)}, u32[]{:S(2)}) copy-start(bf16[32,32,128]{2,1,0:T(8,128)(2,1)} %param.9) | copy-start | bytes 786436
  88.3 28.4 %copy-start.1 = (bf16[128,640]{1,0:T(8,128)(2,1)S(1)}, bf16[128,640]{1,0:T(8,128)(2,1)}, u32[]{:S(2)}) copy-start(bf16[128,640]{1,0:T(8,128)(2,1)} %w_ref.1) | copy-start | bytes 491524
  88.3 28.4 %copy-start.3 = (f32[128]{0:T(128)S(1)}, f32[128]{0:T(128)}, u32[]{:S(2)}) copy-start(f32[128]{0:T(128)} %param.14) | copy-start | bytes 1540
  115.1 2.7 %collective-permute-start.2 = (bf16[384,128]{1,0:T(8,128)(2,1)S(1)}, bf16[384,128]{1,0:T(8,128)(2,1)S(1)}, u32[]{:S(2)}, u32[]{:S(2)}) collective-permute-start(bf16[384,128]{1,0:T(8,128)(2,1)S(1)} %get-tuple-element.49._), channel_id=1, source_target_pairs={{0,16},{16,0},{1,17},{17,1},{2,18},{18,2},{3,19},{19,3},{4,20},{20... | collective-permute-start | bytes 294920 | tf_op jit(solution)/shard_map/ppermute | solution.py:359
